TPU v7x, 256 devices: a whole 4x4x8 slice. The times are simulated.
256 devices in a mesh: dom: 64 (over z, x, core), blk: 4 (over y).
Axes of the slice: x: 4, y: 4, z: 8, core: 2. Of those that a mesh axis runs over, the one named last changes fastest.
Arguments:
- residual: float32 [4096, 135], P(('dom', 'blk')), may hold values from -112.5 to 112.5
- recycle_basis: float32 [8, 4096, 135], P(None, ('dom', 'blk')), may hold values from -5 to 5
- recycle_images: float32 [8, 4096, 135], P(None, ('dom', 'blk')), may hold values from -5 to 5
- jacobian: float32 [4096, 7, 135, 135], P(('dom', 'blk')), may hold values from -1.5 to 5.5
- neighbours: int32 [4096, 6], P(('dom', 'blk')), may hold values from -1 to 4095, as said below
- line_members: int32 [512, 8], replicated, may hold values from 0 to 4095, as said below
- line_pivots: float32 [512, 8, 135, 135], P(('dom', 'blk')), may hold values from -0.2 to 0.4
- line_lower: float32 [512, 7, 135, 135], P(('dom', 'blk')), may hold values from -0.375 to 0.375
- line_upper: float32 [512, 7, 135, 135], P(('dom', 'blk')), may hold values from -0.125 to 0.125
Outputs:
- correction: float32 [4096, 135], P(('dom', 'blk'))
- basis: float32 [9, 4096, 135], P(None, ('dom', 'blk'))
- hessenberg: float32 [9, 8], replicated
- residual_norm: float32 [], replicated
Inputs may be any that keep to these rules, and one draw needn't show every extreme that they name: `line_members`: each element lies in exactly one line. The lines of partition p (the 64 elements p * 64 to (p+1) * 64 - 1 on dom index p) are lines p * 8 onwards; they take exactly 8 elements from partition p-1, exactly 8 from partition p+1 (the first and last partition counting as beside each other) and all others from partition p. `neighbours`: every face neighbour lies in the element's own partition or in one of the two partitions beside it along dom, the first and last partition counting as beside each other.
All inputs are finite; a program needn't handle non-finite values.
Results may differ from a plain program's by a relative error of at most 0.0055.
Values sent between devices are 32-bit elements; how exact they have to be, the bound alone decides.
No kernel may reach another device: no remote copies, remote signals or barrier semaphores. Data moves between devices by JAX's collectives and lax.ppermute only.
A program may use at most 128 MiB of HBM per device.

v0:
```python
import functools

import jax
import jax.numpy as jnp
from jax import lax
from jax.experimental import pallas as pl
from jax.experimental.pallas import tpu as pltpu
from jax.sharding import PartitionSpec as P

STEPS = 8
EPS = 1e-06
LANES = 128
ROWS = 136
INTERPRET = False
f32 = jnp.float32
bf16 = jnp.bfloat16
MIB = 1024 * 1024


def vmem_out(shape):
    if INTERPRET:
        return jax.ShapeDtypeStruct(shape, f32)
    return pltpu.VMEM(shape, f32)


def in_vmem(array):
    return array if INTERPRET else pltpu.with_memory_space_constraint(array, pltpu.VMEM)


def call(body, out_shape, *args, scratch=(), limit=24, specs=None):
    spec = pl.BlockSpec(memory_space=pltpu.VMEM)
    outs = out_shape if isinstance(out_shape, (list, tuple)) else None
    return pl.pallas_call(
        body,
        out_shape=out_shape,
        in_specs=specs if specs is not None else [spec] * len(args),
        out_specs=[spec] * len(outs) if outs is not None else spec,
        scratch_shapes=list(scratch),
        compiler_params=pltpu.CompilerParams(vmem_limit_bytes=limit * MIB),
        interpret=INTERPRET,
    )(*args)


def pick(hits, pool):
    hits = hits.astype(bf16)
    high = pool.astype(bf16)
    rest = pool - high.astype(f32)
    mid = rest.astype(bf16)
    low = (rest - mid.astype(f32)).astype(bf16)
    dot = functools.partial(jnp.dot, preferred_element_type=f32)
    return dot(hits, high) + (dot(hits, mid) + dot(hits, low))


def halves(array):
    high = array.astype(bf16)
    return high, (array - high.astype(f32)).astype(bf16)


def product(left, right, dims):
    lh, ll = halves(left)
    rh, rl = halves(right)
    dot = lambda a, b: lax.dot_general(a, b, (dims, ((), ())), preferred_element_type=f32)
    return dot(lh, rh) + (dot(lh, rl) + dot(ll, rh))


def pack_body(jac_hbm, main_ref, rest_ref):
    faces, rows, elems, cols = jac_hbm.shape
    chunk = 27
    extra = cols - LANES

    def step(block, at=None):
        at = (pl.program_id(0) if at is None else at) * chunk
        lane = lax.broadcasted_iota(jnp.int32, (elems, LANES), 1)

        def row(i, _):
            packed = jnp.zeros((elems, LANES), f32)
            for f in range(faces):
                main_ref[f, at + i] = block[f, i, :, 0:LANES]
                tail = jnp.concatenate(
                    [block[f, i, :, LANES:cols], jnp.zeros((elems, LANES - extra), f32)], 1
                )
                if f:
                    tail = pltpu.roll(tail, f * extra, 1)
                packed = packed + tail
            rest_ref[at + i] = packed
            return 0

        lax.fori_loop(0, chunk, row, 0)

    if INTERPRET:
        for c in range(rows // chunk):
            step(jac_hbm[:, c * chunk : (c + 1) * chunk], c)
        return
    pltpu.emit_pipeline(
        step,
        grid=(rows // chunk,),
        in_specs=[pl.BlockSpec((faces, chunk, elems, cols), lambda c: (0, c, 0, 0))],
    )(jac_hbm)


def invert_body(pivot_ref, lower_ref, upper_ref, main_ref, rest_ref, part_ref, wide_ref, side_ref):
    lines, levels, height, _ = main_ref.shape
    cols = part_ref.shape[2]
    extra = cols - LANES
    rows_by_rows = ((1,), (1,))
    rows_by_cols = ((1,), (0,))
    pivot_rows, pair_rows = levels * cols, lines * cols

    def line(l, _):
        wide_ref[0:pivot_rows, :] = pivot_ref[l, :, 0:LANES]
        side_ref[0:pivot_rows, 0:extra] = pivot_ref[l, :, LANES:cols]

        def strided(first, count):
            at = pl.ds(first, cols, stride=count)
            return jnp.concatenate([wide_ref[at, :], side_ref[at, :][:, 0:extra]], 1)

        def pivot_of(k):
            return strided(k, levels)

        def paired(ref, k):
            wide_ref[pivot_rows:, :] = ref[k, :, 0:LANES]
            side_ref[pivot_rows:, 0:extra] = ref[k, :, LANES:cols]
            return strided(pivot_rows + l, lines)

        part_ref[...] = jnp.zeros(part_ref.shape, f32)
        part_ref[0, 0:cols, :] = pivot_of(0).T

        def forward(k, _):
            pivot = pivot_of(k)
            mixed = product(pivot, paired(lower_ref, k - 1), rows_by_cols)
            part_ref[k] = -product(part_ref[k - 1], mixed, rows_by_rows)
            part_ref[k, pl.ds(pl.multiple_of(k * ROWS, 8), cols), :] = pivot.T
            return 0

        lax.fori_loop(1, levels, forward, 0)

        def backward(i, _):
            k = levels - 2 - i
            part_ref[k] = part_ref[k] - product(
                part_ref[k + 1], paired(upper_ref, k), rows_by_rows
            )
            return 0

        lax.fori_loop(0, levels - 1, backward, 0)

        def emit(t, _):
            at = pl.ds(pl.multiple_of(t * ROWS, 8), ROWS)
            packed = jnp.zeros((ROWS, LANES), f32)
            for k in range(levels):
                main_ref[l, k, at, :] = part_ref[k, at, 0:LANES]
                tail = jnp.concatenate(
                    [part_ref[k, at, LANES:cols], jnp.zeros((ROWS, LANES - extra), f32)], 1
                )
                packed = packed + (pltpu.roll(tail, k * extra, 1) if k else tail)
            rest_ref[l, at, :] = packed
            return 0

        lax.fori_loop(0, levels, emit, 0)
        return 0

    lax.fori_loop(0, lines, line, 0)


def solve_body(*refs):
    *blocks, hits_ref, main_ref, rest_ref, out_ref, pool_ref, wide_ref = refs
    lines, levels, height, _ = main_ref.shape
    count = hits_ref.shape[0]
    cols = pool_ref.shape[1]
    extra = cols - LANES
    fill_pool(blocks, pool_ref)
    rhs = pick(hits_ref[...], pool_ref[...])
    rhs = jnp.concatenate([rhs, jnp.zeros((count, 2 * LANES - cols), f32)], 1)
    rhs = rhs.T[0:ROWS]
    for q in range(count):
        wide_ref[q] = jnp.broadcast_to(rhs[:, q : q + 1], (ROWS, LANES))
    for l in range(lines):

        def member(m, sums):
            sums = list(sums)
            for t in range(ROWS // 8):
                at = pl.ds(pl.multiple_of(m * ROWS + t * 8, 8), 8)
                value = wide_ref[l * levels + m, t * 8 : t * 8 + 8, :]
                for k in range(levels):
                    sums[k] = sums[k] + main_ref[l, k, at, :] * value
                sums[levels] = sums[levels] + rest_ref[l, at, :] * value
            return tuple(sums)

        zero = jnp.zeros((8, LANES), f32)
        sums = lax.fori_loop(0, levels, member, (zero,) * (levels + 1))
        tails = jnp.sum(sums[levels], axis=0, keepdims=True)
        tails = jnp.broadcast_to(tails, (8, LANES))
        for k in range(levels):
            at = slice(l * levels + k, l * levels + k + 1)
            out_ref[at, 0:LANES] = jnp.sum(sums[k], axis=0, keepdims=True)
            tail = pltpu.roll(tails, LANES - k * extra, 1) if k else tails
            out_ref[at, LANES:cols] = tail[0:1, 0:extra]


def fill_pool(blocks, pool_ref):
    at = 0
    for block in blocks:
        count = block.shape[0]
        pool_ref[at : at + count, :] = block[...]
        at += count


def operate(blocks, hits_ref, main_ref, rest_ref, pool_ref):
    faces, rows, elems, _ = main_ref.shape
    cols = pool_ref.shape[1]
    extra = cols - LANES
    fill_pool(blocks, pool_ref)
    field = pick(hits_ref[...], pool_ref[...])
    heads = [field[f * elems : (f + 1) * elems, 0:LANES] for f in range(faces)]
    packed = jnp.zeros((elems, LANES), f32)
    for f in range(faces):
        tail = jnp.concatenate(
            [field[f * elems : (f + 1) * elems, LANES:cols], jnp.zeros((elems, LANES - extra), f32)], 1
        )
        packed = packed + (pltpu.roll(tail, f * extra, 1) if f else tail)
    lane = lax.broadcasted_iota(jnp.int32, (elems, LANES), 1)

    def one(i):
        total = rest_ref[i] * packed
        for f in range(faces):
            total = total + main_ref[f, i] * heads[f]
        return jnp.sum(total, axis=1, keepdims=True)

    group = 16

    def some(g, image):
        for s in range(group):
            i = g * group + s
            image = jnp.where(lane == i, one(i), image)
        return image

    image = lax.fori_loop(0, LANES // group, some, jnp.zeros((elems, LANES), f32))
    tail = jnp.zeros((elems, LANES), f32)
    for c in range(extra):
        tail = jnp.where(lane == c, one(LANES + c), tail)
    return jnp.concatenate([image, tail[:, 0:extra]], 1)


def row_of(values):
    lane = lax.broadcasted_iota(jnp.int32, (1, LANES), 1)
    row = jnp.zeros((1, LANES), f32)
    for i, value in values.items():
        total = jnp.sum(jnp.sum(value, axis=0, keepdims=True), axis=1, keepdims=True)
        row = jnp.where(lane == i, total, row)
    return row


def lane_of(row, i):
    return row[:, i : i + 1]


UC, UU, CC = 13, 14, 15
SHIFT, SCALE, STEP = 0, 1, 2


def totals(parts_ref):
    return jnp.sum(parts_ref[...], axis=0, keepdims=True)


def project_body(images_ref, residual_ref, out_ref):
    residual = residual_ref[...]
    out_ref[...] = row_of({k: images_ref[k] * residual for k in range(images_ref.shape[0])})


def deflate_body(entries, parts_ref, residual_ref, basis_ref, images_ref, correction_ref, start_ref):
    row = totals(parts_ref) / entries
    correction = jnp.zeros(residual_ref.shape, f32)
    start = residual_ref[...]
    for k in range(basis_ref.shape[0]):
        weight = lane_of(row, k)
        correction = correction + weight * basis_ref[k]
        start = start - weight * images_ref[k]
    correction_ref[...] = correction
    start_ref[...] = start


def first_body(*refs):
    *blocks, u_ref, hits_ref, main_ref, rest_ref, c_ref, part_ref, pool_ref = refs
    c = operate(blocks, hits_ref, main_ref, rest_ref, pool_ref)
    c_ref[...] = c
    u = u_ref[...]
    part_ref[...] = row_of({UC: u * c, UU: u * u, CC: c * c})


def advance(entries, row, u, c, known, basis):
    scale, step = lane_of(known, SCALE), lane_of(known, STEP)
    norm = jnp.sqrt(lane_of(row, UU) / entries + EPS / (scale * scale))
    inverse = 1.0 / norm
    here = u * inverse
    image = c * inverse
    lane = lax.broadcasted_iota(jnp.int32, (1, LANES), 1)
    own = lane_of(row, UC) * inverse * inverse / entries
    column = jnp.where(lane < STEPS, row * inverse / entries, 0.0)
    column = jnp.where(lane.astype(f32) == step, own, column)
    scale_next = jnp.sqrt(lane_of(row, CC) * inverse * inverse / entries + EPS)
    reduced = image - own * here
    for i in range(STEPS):
        reduced = reduced - lane_of(row, i) * inverse / entries * basis[i]
    return here, image, inverse, own, column, scale * norm, reduced / scale_next, scale_next


def place(out_ref, in_ref, step, value):
    for i in range(in_ref.shape[0]):
        out_ref[i] = jnp.where(step == i, value, in_ref[i])


def record(hess_out, hess_ref, step, column, below):
    at = lax.broadcasted_iota(jnp.int32, hess_ref.shape, 0).astype(f32)
    lane = lax.broadcasted_iota(jnp.int32, hess_ref.shape, 1).astype(f32)
    hess = jnp.where(at == step, column, hess_ref[...])
    hess_out[...] = jnp.where((at == STEPS) & (lane == step), below, hess)


def numbers(shift, scale, step):
    lane = lax.broadcasted_iota(jnp.int32, (1, LANES), 1)
    row = jnp.where(lane == SHIFT, shift, jnp.zeros((1, LANES), f32))
    row = jnp.where(lane == SCALE, scale, row)
    return jnp.where(lane == STEP, step, row)


def next_body(entries, *refs):
    *blocks, hits_ref, main_ref, rest_ref, sums_ref, u_ref, c_ref, known_ref = refs[:-12]
    basis_ref, images_ref, hess_ref, basis_out, images_out, hess_out = refs[-12:-6]
    u_out, c_out, v_out, known_out, part_ref, pool_ref = refs[-6:]
    w = operate(blocks, hits_ref, main_ref, rest_ref, pool_ref)
    known = known_ref[...]
    step = lane_of(known, STEP)
    row = totals(sums_ref)
    here, image, inverse, own, column, below, u, scale = advance(
        entries, row, u_ref[...], c_ref[...], known, basis_ref
    )
    moved = w * inverse - (own - lane_of(known, SHIFT)) * image
    for i in range(STEPS):
        moved = moved - lane_of(row, i) * inverse / entries * images_ref[i]
    c = moved / scale
    place(basis_out, basis_ref, step, here)
    place(images_out, images_ref, step, image)
    record(hess_out, hess_ref, step, column, below)
    u_out[...] = u
    c_out[...] = c
    v_out[...] = c - own * u
    known_out[...] = numbers(own, scale, step + 1.0)
    products = {i: jnp.where(step == i, here, basis_ref[i]) * c for i in range(STEPS)}
    products.update({UC: u * c, UU: u * u, CC: c * c})
    part_ref[...] = row_of(products)


def last_body(entries, sums_ref, u_ref, c_ref, known_ref, basis_ref, hess_ref, *outs):
    basis_out, hess_out, u_out, known_out, part_ref = outs
    known = known_ref[...]
    step = lane_of(known, STEP)
    here, _, _, own, column, below, u, scale = advance(
        entries, totals(sums_ref), u_ref[...], c_ref[...], known, basis_ref
    )
    place(basis_out, basis_ref, step, here)
    record(hess_out, hess_ref, step, column, below)
    u_out[...] = u
    known_out[...] = numbers(own, scale, step + 1.0)
    part_ref[...] = row_of({UU: u * u})


def finish_body(entries, sums_ref, u_ref, known_ref, basis_ref, hess_ref, basis_out, hess_out, norm_ref):
    scale = lane_of(known_ref[...], SCALE)
    norm = jnp.sqrt(lane_of(totals(sums_ref), UU) / entries + EPS / (scale * scale))
    for i in range(STEPS):
        basis_out[i] = basis_ref[i]
    basis_out[STEPS] = u_ref[...] / norm
    lane = lax.broadcasted_iota(jnp.int32, (1, LANES), 1)
    norms = hess_ref[STEPS : STEPS + 1, :]
    for j in range(STEPS):
        below = lane_of(norms, j + 1) if j + 1 < STEPS else scale * norm
        hess_out[j : j + 1, :] = jnp.where(lane == j + 1, below, hess_ref[j : j + 1, :])
    norm_ref[...] = norms


def shifted(array, d_dom, d_blk):
    doms, blks = lax.axis_size("dom"), lax.axis_size("blk")
    if d_dom == 0 and d_blk == 0:
        return array
    pairs = []
    for d in range(doms):
        for b in range(blks):
            source = ((d + d_dom) % doms) * blks + (b + d_blk) % blks
            pairs.append((source, d * blks + b))
    return lax.ppermute(array, ("dom", "blk"), pairs)


def partition(array):
    return [shifted(array, 0, b) for b in range(lax.axis_size("blk"))]


def near_rows(array):
    blks = lax.axis_size("blk")
    return [shifted(array, d, b) for d in (-1, 0, 1) for b in range(blks)]


def far_rows(array):
    whole = jnp.concatenate(partition(array), 0)
    return [shifted(whole, d, 0) for d in (-2, -1, 0, 1, 2)]


def gathered(part):
    return lax.all_gather(part, ("dom", "blk"), axis=0, tiled=True)


def added(part):
    doms, blks = lax.axis_size("dom"), lax.axis_size("blk")
    devices = doms * blks
    reach = 1
    while reach < devices:
        ways = 4 if reach * 4 <= devices else 2
        others = [
            lax.ppermute(part, ("dom", "blk"), [(n ^ (k * reach), n) for n in range(devices)])
            for k in range(1, ways)
        ]
        if ways == 4:
            part = (part + others[0]) + (others[1] + others[2])
        else:
            part = part + others[0]
        reach *= ways
    return part


def per_device(residual, recycle_basis, recycle_images, jacobian, neighbours, line_members,
               line_pivots, line_lower, line_upper):
    elems, cols = residual.shape
    doms, blks = lax.axis_size("dom"), lax.axis_size("blk")
    faces = jacobian.shape[1]
    lines, levels = line_pivots.shape[:2]
    entries = float(elems * cols * doms * blks)
    dom, blk = lax.axis_index("dom"), lax.axis_index("blk")
    devices = doms * blks

    row = jax.ShapeDtypeStruct((1, LANES), f32)
    rows = jax.ShapeDtypeStruct((elems, cols), f32)
    projected = added(call(project_body, row, recycle_images, residual))

    members = line_members.reshape(devices, elems)
    near = jnp.array([(d, b) for d in range(-2, 3) for b in range(blks)], jnp.int32)
    at = (dom + near[:, 0] + doms) % doms * blks + (blk + near[:, 1]) % blks
    line_ids = members[at].reshape(-1)
    near_own = at[blks : 4 * blks]
    elem_ids = (near_own[:, None] * elems + jnp.arange(elems, dtype=jnp.int32)).reshape(-1)
    me = dom * blks + blk
    own_ids = me * elems + jnp.arange(elems, dtype=jnp.int32)
    wanted = jnp.concatenate([own_ids[None], neighbours.T], 0).reshape(-1)
    stencil = (wanted[:, None] == line_ids[None, :]).astype(f32)
    mine = lax.dynamic_slice_in_dim(members, me, 1, 0)[0]
    entering = (mine[:, None] == elem_ids[None, :]).astype(f32)

    spec = pl.BlockSpec(memory_space=pltpu.VMEM)
    hbm = pl.BlockSpec(memory_space=pl.ANY)
    jac = jnp.transpose(jacobian, (1, 2, 0, 3))
    jac_main, jac_rest = call(
        pack_body,
        [vmem_out((faces, cols, elems, LANES)), vmem_out((cols, elems, LANES))],
        jac,
        specs=[spec if INTERPRET else hbm],
        limit=24,
    )
    pivots = jnp.transpose(line_pivots, (0, 2, 1, 3)).reshape(lines, cols * levels, cols)
    lower = jnp.transpose(line_lower, (1, 2, 0, 3)).reshape(levels - 1, cols * lines, cols)
    upper = jnp.transpose(line_upper, (1, 2, 0, 3)).reshape(levels - 1, cols * lines, cols)
    height = levels * ROWS
    inv_main, inv_rest = call(
        invert_body,
        [vmem_out((lines, levels, height, LANES)), vmem_out((lines, height, LANES))],
        pivots,
        lower,
        upper,
        scratch=[
            pltpu.VMEM((levels, height, cols), f32),
            pltpu.VMEM(((levels + lines) * cols, LANES), f32),
            pltpu.VMEM(((levels + lines) * cols, LANES), f32),
        ],
        limit=40,
    )
    jac_main, jac_rest, inv_main, inv_rest = map(in_vmem, (jac_main, jac_rest, inv_main, inv_rest))

    correction, u = call(
        functools.partial(deflate_body, entries),
        [rows, rows],
        projected,
        residual,
        recycle_basis,
        recycle_images,
    )

    def precondition(v):
        z = call(
            solve_body,
            rows,
            *near_rows(v),
            entering,
            inv_main,
            inv_rest,
            scratch=[
                pltpu.VMEM((entering.shape[1], cols), f32),
                pltpu.VMEM((elems, ROWS, LANES), f32),
            ],
        )
        return far_rows(z)

    stencil_pool = pltpu.VMEM((stencil.shape[1], cols), f32)
    matrices = (stencil, jac_main, jac_rest)
    c, part = call(
        first_body, [rows, row], *precondition(u), u, *matrices, scratch=[stencil_pool]
    )
    stack = jax.ShapeDtypeStruct((STEPS, elems, cols), f32)
    hess = jax.ShapeDtypeStruct((2 * STEPS, LANES), f32)

    def step(_, state):
        basis, images, hessenberg, u, c, v, known, part = state
        return tuple(
            call(
                functools.partial(next_body, entries),
                [stack, stack, hess, rows, rows, rows, row, row],
                *precondition(v),
                *matrices,
                gathered(part),
                u,
                c,
                known,
                basis,
                images,
                hessenberg,
                scratch=[stencil_pool],
            )
        )

    empty = jnp.zeros(stack.shape, f32)
    known = jnp.zeros((1, LANES), f32).at[0, SCALE].set(1.0)
    state = (empty, empty, jnp.zeros(hess.shape, f32), u, c, c, known, part)
    basis, _, hessenberg, u, c, _, known, part = lax.fori_loop(0, STEPS - 1, step, state)
    basis, hessenberg, u, known, part = call(
        functools.partial(last_body, entries),
        [stack, hess, rows, row, row],
        added(part),
        u,
        c,
        known,
        basis,
        hessenberg,
    )
    basis, hessenberg, norm = call(
        functools.partial(finish_body, entries),
        [
            jax.ShapeDtypeStruct((STEPS + 1, elems, cols), f32),
            jax.ShapeDtypeStruct((STEPS, LANES), f32),
            row,
        ],
        added(part),
        u,
        known,
        basis,
        hessenberg,
    )
    return correction, basis, hessenberg[:, : STEPS + 1].T, norm[0, 0]


def solution(mesh):
    both = ("dom", "blk")
    in_specs = (
        P(both, None),
        P(None, both, None),
        P(None, both, None),
        P(both, None, None, None),
        P(both, None),
        P(),
        P(both, None, None, None),
        P(both, None, None, None),
        P(both, None, None, None),
    )
    out_specs = (P(both, None), P(None, both, None), P(), P())
    return jax.shard_map(
        per_device, mesh=mesh, in_specs=in_specs, out_specs=out_specs, check_vma=False
    )
```

profile of v0, /device:TPU:68, one launch (start us, length us, event | category | flops | bytes accessed | tf_op | source)
XLA Modules:
  0.0 898.4 jit_solution(9315234643129992930)
XLA Ops:
  2.4 3.1 collective-permute-start.20
  7.3 3.1 collective-permute-done.19
  16.3 3.0 collective-permute-start.24
  21.4 4.5 collective-permute-start.29
  28.4 4.9 collective-permute-done.28
  37.2 4.0 collective-permute-start.39
  57.4 3.5 reshape.90.upper_ref
  62.4 29.0 %shard_map.131 = (f32[2,8,1088,128]{3,2,1,0:T(8,128)S(1)}, f32[2,1088,128]{2,1,0:T(8,128)S(1)}) custom-call(f32[2,1080,135]{2,1,0:T(8,128)} %bitcast.39, f32[7,270,135]{2,1,0:T(8,128)S(1)} %reshape.89.lower_ref, f32[7,270,135]{2,1,0:T(8,128)S(1)} %copy-done.6), custom_call_target="tpu_custom_call" | custom-call | tf_op jit(solution)/shard_map/pallas_call | solution.py:33
  104.4 5.4 copy-done.5
  109.8 12.1 %shard_map.133 = (f32[7,135,16,128]{3,2,1,0:T(8,128)S(1)}, f32[135,16,128]{2,1,0:T(8,128)S(1)}) custom-call(f32[7,135,16,135]{3,2,1,0:T(8,128)S(1)} %bitcast.37), custom_call_target="tpu_custom_call" | custom-call | tf_op jit(solution)/shard_map/pallas_call | solution.py:33
  121.9 3.1 copy-done.2
  127.1 3.2 copy-done.3
  132.0 705.6 %while.26 = (s32[]{:T(128)}, f32[8,16,135]{2,1,0:T(8,128)S(1)}, f32[8,16,135]{2,1,0:T(8,128)S(1)}, f32[16,128]{1,0:T(8,128)S(1)}, f32[16,135]{1,0:T(8,128)S(1)},...) while((s32[]{:T(128)}, f32[8,16,135]{2,1,0:T(8,128)S(1)}, ...), condition=%wide.region_2.3_spmd.clone, body=%wide.region_1.2_spmd.clone.sunk | while | flops 103746 | bytes 68342440 | solution.py:538
  142.4 3.8 collective-permute-start.8
  151.6 3.2 collective-permute-start.2
  157.3 3.7 collective-permute-start
  161.9 3.5 collective-permute-done.10.refs_11_
  165.8 3.5 copy-done.1
  181.2 59.3 %all-gather.3 = f32[256,1,128]{2,1,0:T(1,128)S(1)} all-gather(f32[1,1,128]{2,1,0:T(1,128)S(1)} %bitcast.42), channel_id=1, replica_groups=mesh['dom'=64,'blk'=4] {'dom','blk'}, dimensions={0}, use_global_device_ids=true | all-gather | bytes 131584 | tf_op jit(solution)/shard_map/while/body/eval_jaxpr/all_gather | solution.py:407
  240.5 3.2 copy-done.4
  254.3 3.6 collective-permute-start.1
  257.9 3.3 collective-permute-start
  262.1 3.5 collective-permute-done.10.refs_11_
  266.1 3.5 copy-done.1
  279.5 3.7 collective-permute-start.14
  283.2 55.7 %all-gather.3 = f32[256,1,128]{2,1,0:T(1,128)S(1)} all-gather(f32[1,1,128]{2,1,0:T(1,128)S(1)} %bitcast.42), channel_id=1, replica_groups=mesh['dom'=64,'blk'=4] {'dom','blk'}, dimensions={0}, use_global_device_ids=true | all-gather | bytes 131584 | tf_op jit(solution)/shard_map/while/body/eval_jaxpr/all_gather | solution.py:407
  339.0 3.2 copy-done.4
  352.7 3.5 collective-permute-start.1
  356.3 3.6 collective-permute-start
  360.7 3.5 collective-permute-done.10.refs_11_
  364.7 3.5 copy-done.1
  378.0 3.7 collective-permute-start.14
  381.7 56.2 %all-gather.3 = f32[256,1,128]{2,1,0:T(1,128)S(1)} all-gather(f32[1,1,128]{2,1,0:T(1,128)S(1)} %bitcast.42), channel_id=1, replica_groups=mesh['dom'=64,'blk'=4] {'dom','blk'}, dimensions={0}, use_global_device_ids=true | all-gather | bytes 131584 | tf_op jit(solution)/shard_map/while/body/eval_jaxpr/all_gather | solution.py:407
  438.0 3.2 copy-done.4
  451.7 4.1 collective-permute-start.1
  459.6 3.5 collective-permute-done.10.refs_11_
  463.5 3.5 copy-done.1
  476.9 3.7 collective-permute-start.14
  480.5 55.6 %all-gather.3 = f32[256,1,128]{2,1,0:T(1,128)S(1)} all-gather(f32[1,1,128]{2,1,0:T(1,128)S(1)} %bitcast.42), channel_id=1, replica_groups=mesh['dom'=64,'blk'=4] {'dom','blk'}, dimensions={0}, use_global_device_ids=true | all-gather | bytes 131584 | tf_op jit(solution)/shard_map/while/body/eval_jaxpr/all_gather | solution.py:407
  536.2 3.2 copy-done.4
  550.0 4.1 collective-permute-start.1
  554.1 2.9 collective-permute-start
  557.8 3.5 collective-permute-done.10.refs_11_
  561.8 3.5 copy-done.1
  575.1 3.7 collective-permute-start.14
  578.8 56.3 %all-gather.3 = f32[256,1,128]{2,1,0:T(1,128)S(1)} all-gather(f32[1,1,128]{2,1,0:T(1,128)S(1)} %bitcast.42), channel_id=1, replica_groups=mesh['dom'=64,'blk'=4] {'dom','blk'}, dimensions={0}, use_global_device_ids=true | all-gather | bytes 131584 | tf_op jit(solution)/shard_map/while/body/eval_jaxpr/all_gather | solution.py:407
  635.1 3.2 copy-done.4
  648.9 4.1 collective-permute-start.1
  656.7 3.5 collective-permute-done.10.refs_11_
  660.7 3.5 copy-done.1
  674.0 3.7 collective-permute-start.14
  677.7 55.8 %all-gather.3 = f32[256,1,128]{2,1,0:T(1,128)S(1)} all-gather(f32[1,1,128]{2,1,0:T(1,128)S(1)} %bitcast.42), channel_id=1, replica_groups=mesh['dom'=64,'blk'=4] {'dom','blk'}, dimensions={0}, use_global_device_ids=true | all-gather | bytes 131584 | tf_op jit(solution)/shard_map/while/body/eval_jaxpr/all_gather | solution.py:407
  733.6 3.2 copy-done.4
  747.3 4.1 collective-permute-start.1
  751.5 2.8 collective-permute-start
  755.2 3.5 collective-permute-done.10.refs_11_
  759.1 3.5 copy-done.1
  772.5 3.7 collective-permute-start.14
  776.1 56.1 %all-gather.3 = f32[256,1,128]{2,1,0:T(1,128)S(1)} all-gather(f32[1,1,128]{2,1,0:T(1,128)S(1)} %bitcast.42), channel_id=1, replica_groups=mesh['dom'=64,'blk'=4] {'dom','blk'}, dimensions={0}, use_global_device_ids=true | all-gather | bytes 131584 | tf_op jit(solution)/shard_map/while/body/eval_jaxpr/all_gather | solution.py:407
  832.3 3.2 copy-done.4
  849.9 4.1 collective-permute-start.56
  861.1 3.1 collective-permute-start.58
  889.1 2.9 collective-permute-start.70
  893.6 3.0 collective-permute-done.70
  (480 shorter events, 256.8 us)
Async XLA Ops:
  37.2 8.7 collective-permute-start.39
  44.4 8.0 collective-permute-start.35
  45.9 45.5 %collective-permute-start.34 = (f32[16,135]{1,0:T(8,128)S(1)}, f32[16,135]{1,0:T(8,128)S(1)}, u32[]{:S(2)}, u32[]{:S(2)}) collective-permute-start(f32[16,135]{1,0:T(8,128)S(1)} %get-tuple-element.350.refs_4_.refs_5_), channel_id=1, source_target_pairs={{1,0},{2,1},{3,2},{0,3},{5,4},{6,5},{7,6},{4,7},{9,8},{10,9},{11,1... | collective-permute-start | bytes 25928 | tf_op jit(solution)/shard_map/ppermute | solution.py:389
  48.6 42.9 %collective-permute-start.33 = (f32[16,135]{1,0:T(8,128)S(1)}, f32[16,135]{1,0:T(8,128)S(1)}, u32[]{:S(2)}, u32[]{:S(2)}) collective-permute-start(f32[16,135]{1,0:T(8,128)S(1)} %get-tuple-element.350.refs_4_.refs_5_), channel_id=1, source_target_pairs={{255,0},{252,1},{253,2},{254,3},{3,4},{0,5},{1,6},{2,7},{7,8},{4,9... | collective-permute-start | bytes 25928 | tf_op jit(solution)/shard_map/ppermute | solution.py:389
  48.9 42.6 %collective-permute-start.32 = (f32[16,135]{1,0:T(8,128)S(1)}, f32[16,135]{1,0:T(8,128)S(1)}, u32[]{:S(2)}, u32[]{:S(2)}) collective-permute-start(f32[16,135]{1,0:T(8,128)S(1)} %get-tuple-element.350.refs_4_.refs_5_), channel_id=1, source_target_pairs={{254,0},{255,1},{252,2},{253,3},{2,4},{3,5},{0,6},{1,7},{6,8},{7,9... | collective-permute-start | bytes 25928 | tf_op jit(solution)/shard_map/ppermute | solution.py:389
  50.2 41.3 %collective-permute-start.31 = (f32[16,135]{1,0:T(8,128)S(1)}, f32[16,135]{1,0:T(8,128)S(1)}, u32[]{:S(2)}, u32[]{:S(2)}) collective-permute-start(f32[16,135]{1,0:T(8,128)S(1)} %get-tuple-element.350.refs_4_.refs_5_), channel_id=1, source_target_pairs={{253,0},{254,1},{255,2},{252,3},{1,4},{2,5},{3,6},{0,7},{5,8},{6,9... | collective-permute-start | bytes 25928 | tf_op jit(solution)/shard_map/ppermute | solution.py:389
  52.5 39.0 %collective-permute-start.30 = (f32[16,135]{1,0:T(8,128)S(1)}, f32[16,135]{1,0:T(8,128)S(1)}, u32[]{:S(2)}, u32[]{:S(2)}) collective-permute-start(f32[16,135]{1,0:T(8,128)S(1)} %get-tuple-element.350.refs_4_.refs_5_), channel_id=1, source_target_pairs={{252,0},{253,1},{254,2},{255,3},{0,4},{1,5},{2,6},{3,7},{4,8},{5,9... | collective-permute-start | bytes 25928 | tf_op jit(solution)/shard_map/ppermute | solution.py:389
  100.9 26.1 %collective-permute-start.47 = (f32[64,135]{1,0:T(8,128)S(1)}, f32[64,135]{1,0:T(8,128)S(1)}, u32[]{:S(2)}, u32[]{:S(2)}) collective-permute-start(f32[64,135]{1,0:T(8,128)S(1)} %pad_maximum_fusion.1.refs_2_), channel_id=1, source_target_pairs={{8,0},{9,1},{10,2},{11,3},{12,4},{13,5},{14,6},{15,7},{16,8},{17,9... | collective-permute-start | bytes 103688 | tf_op jit(solution)/shard_map/ppermute | solution.py:389
  101.0 26.0 %collective-permute-start.46 = (f32[64,135]{1,0:T(8,128)S(1)}, f32[64,135]{1,0:T(8,128)S(1)}, u32[]{:S(2)}, u32[]{:S(2)}) collective-permute-start(f32[64,135]{1,0:T(8,128)S(1)} %pad_maximum_fusion.1.refs_2_), channel_id=1, source_target_pairs={{4,0},{5,1},{6,2},{7,3},{8,4},{9,5},{10,6},{11,7},{12,8},{13,9},{1... | collective-permute-start | bytes 103688 | tf_op jit(solution)/shard_map/ppermute | solution.py:389
  101.1 26.0 %collective-permute-start.45 = (f32[64,135]{1,0:T(8,128)S(1)}, f32[64,135]{1,0:T(8,128)S(1)}, u32[]{:S(2)}, u32[]{:S(2)}) collective-permute-start(f32[64,135]{1,0:T(8,128)S(1)} %pad_maximum_fusion.1.refs_2_), channel_id=1, source_target_pairs={{252,0},{253,1},{254,2},{255,3},{0,4},{1,5},{2,6},{3,7},{4,8},{5,9... | collective-permute-start | bytes 103688 | tf_op jit(solution)/shard_map/ppermute | solution.py:389
  101.6 25.5 %collective-permute-start.44 = (f32[64,135]{1,0:T(8,128)S(1)}, f32[64,135]{1,0:T(8,128)S(1)}, u32[]{:S(2)}, u32[]{:S(2)}) collective-permute-start(f32[64,135]{1,0:T(8,128)S(1)} %pad_maximum_fusion.1.refs_2_), channel_id=1, source_target_pairs={{248,0},{249,1},{250,2},{251,3},{252,4},{253,5},{254,6},{255,7},{0... | collective-permute-start | bytes 103688 | tf_op jit(solution)/shard_map/ppermute | solution.py:389
  146.1 8.7 collective-permute-start.6
  146.1 11.2 %collective-permute-start.5 = (f32[16,135]{1,0:T(8,128)S(1)}, f32[16,135]{1,0:T(8,128)S(1)}, u32[]{:S(2)}, u32[]{:S(2)}) collective-permute-start(f32[16,135]{1,0:T(8,128)S(1)} %get-tuple-element.370.refs_4_), channel_id=1, source_target_pairs={{2,0},{3,1},{0,2},{1,3},{6,4},{7,5},{4,6},{5,7},{10,8},{11,9},{8,1... | collective-permute-start | bytes 25928 | tf_op jit(solution)/shard_map/while/body/eval_jaxpr/ppermute | solution.py:389
  148.2 12.8 %collective-permute-start.4 = (f32[16,135]{1,0:T(8,128)S(1)}, f32[16,135]{1,0:T(8,128)S(1)}, u32[]{:S(2)}, u32[]{:S(2)}) collective-permute-start(f32[16,135]{1,0:T(8,128)S(1)} %get-tuple-element.370.refs_4_), channel_id=1, source_target_pairs={{1,0},{2,1},{3,2},{0,3},{5,4},{6,5},{7,6},{4,7},{9,8},{10,9},{11,1... | collective-permute-start | bytes 25928 | tf_op jit(solution)/shard_map/while/body/eval_jaxpr/ppermute | solution.py:389
  149.5 11.6 %collective-permute-start.3 = (f32[16,135]{1,0:T(8,128)S(1)}, f32[16,135]{1,0:T(8,128)S(1)}, u32[]{:S(2)}, u32[]{:S(2)}) collective-permute-start(f32[16,135]{1,0:T(8,128)S(1)} %get-tuple-element.370.refs_4_), channel_id=1, source_target_pairs={{255,0},{252,1},{253,2},{254,3},{3,4},{0,5},{1,6},{2,7},{7,8},{4,9... | collective-permute-start | bytes 25928 | tf_op jit(solution)/shard_map/while/body/eval_jaxpr/ppermute | solution.py:389
  151.6 9.6 %collective-permute-start.2 = (f32[16,135]{1,0:T(8,128)S(1)}, f32[16,135]{1,0:T(8,128)S(1)}, u32[]{:S(2)}, u32[]{:S(2)}) collective-permute-start(f32[16,135]{1,0:T(8,128)S(1)} %get-tuple-element.370.refs_4_), channel_id=1, source_target_pairs={{254,0},{255,1},{252,2},{253,3},{2,4},{3,5},{0,6},{1,7},{6,8},{7,9... | collective-permute-start | bytes 25928 | tf_op jit(solution)/shard_map/while/body/eval_jaxpr/ppermute | solution.py:389
  178.5 62.0 %collective-permute-start.17 = (f32[64,135]{1,0:T(8,128)S(1)}, f32[64,135]{1,0:T(8,128)S(1)}, u32[]{:S(2)}, u32[]{:S(2)}) collective-permute-start(f32[64,135]{1,0:T(8,128)S(1)} %pad_maximum_fusion.3.refs_2_), channel_id=1, source_target_pairs={{8,0},{9,1},{10,2},{11,3},{12,4},{13,5},{14,6},{15,7},{16,8},{17,9... | collective-permute-start | bytes 103688 | tf_op jit(solution)/shard_map/while/body/eval_jaxpr/ppermute | solution.py:389
  178.5 61.9 %collective-permute-start.16 = (f32[64,135]{1,0:T(8,128)S(1)}, f32[64,135]{1,0:T(8,128)S(1)}, u32[]{:S(2)}, u32[]{:S(2)}) collective-permute-start(f32[64,135]{1,0:T(8,128)S(1)} %pad_maximum_fusion.3.refs_2_), channel_id=1, source_target_pairs={{4,0},{5,1},{6,2},{7,3},{8,4},{9,5},{10,6},{11,7},{12,8},{13,9},{1... | collective-permute-start | bytes 103688 | tf_op jit(solution)/shard_map/while/body/eval_jaxpr/ppermute | solution.py:389
  178.6 61.8 %collective-permute-start.15 = (f32[64,135]{1,0:T(8,128)S(1)}, f32[64,135]{1,0:T(8,128)S(1)}, u32[]{:S(2)}, u32[]{:S(2)}) collective-permute-start(f32[64,135]{1,0:T(8,128)S(1)} %pad_maximum_fusion.3.refs_2_), channel_id=1, source_target_pairs={{252,0},{253,1},{254,2},{255,3},{0,4},{1,5},{2,6},{3,7},{4,8},{5,9... | collective-permute-start | bytes 103688 | tf_op jit(solution)/shard_map/while/body/eval_jaxpr/ppermute | solution.py:389
  179.2 61.3 %collective-permute-start.14 = (f32[64,135]{1,0:T(8,128)S(1)}, f32[64,135]{1,0:T(8,128)S(1)}, u32[]{:S(2)}, u32[]{:S(2)}) collective-permute-start(f32[64,135]{1,0:T(8,128)S(1)} %pad_maximum_fusion.3.refs_2_), channel_id=1, source_target_pairs={{248,0},{249,1},{250,2},{251,3},{252,4},{253,5},{254,6},{255,7},{0... | collective-permute-start | bytes 103688 | tf_op jit(solution)/shard_map/while/body/eval_jaxpr/ppermute | solution.py:389
  251.9 9.3 %collective-permute-start.4 = (f32[16,135]{1,0:T(8,128)S(1)}, f32[16,135]{1,0:T(8,128)S(1)}, u32[]{:S(2)}, u32[]{:S(2)}) collective-permute-start(f32[16,135]{1,0:T(8,128)S(1)} %get-tuple-element.370.refs_4_), channel_id=1, source_target_pairs={{1,0},{2,1},{3,2},{0,3},{5,4},{6,5},{7,6},{4,7},{9,8},{10,9},{11,1... | collective-permute-start | bytes 25928 | tf_op jit(solution)/shard_map/while/body/eval_jaxpr/ppermute | solution.py:389
  278.6 60.3 %collective-permute-start.17 = (f32[64,135]{1,0:T(8,128)S(1)}, f32[64,135]{1,0:T(8,128)S(1)}, u32[]{:S(2)}, u32[]{:S(2)}) collective-permute-start(f32[64,135]{1,0:T(8,128)S(1)} %pad_maximum_fusion.3.refs_2_), channel_id=1, source_target_pairs={{8,0},{9,1},{10,2},{11,3},{12,4},{13,5},{14,6},{15,7},{16,8},{17,9... | collective-permute-start | bytes 103688 | tf_op jit(solution)/shard_map/while/body/eval_jaxpr/ppermute | solution.py:389
  278.7 60.2 %collective-permute-start.16 = (f32[64,135]{1,0:T(8,128)S(1)}, f32[64,135]{1,0:T(8,128)S(1)}, u32[]{:S(2)}, u32[]{:S(2)}) collective-permute-start(f32[64,135]{1,0:T(8,128)S(1)} %pad_maximum_fusion.3.refs_2_), channel_id=1, source_target_pairs={{4,0},{5,1},{6,2},{7,3},{8,4},{9,5},{10,6},{11,7},{12,8},{13,9},{1... | collective-permute-start | bytes 103688 | tf_op jit(solution)/shard_map/while/body/eval_jaxpr/ppermute | solution.py:389
  278.8 60.1 %collective-permute-start.15 = (f32[64,135]{1,0:T(8,128)S(1)}, f32[64,135]{1,0:T(8,128)S(1)}, u32[]{:S(2)}, u32[]{:S(2)}) collective-permute-start(f32[64,135]{1,0:T(8,128)S(1)} %pad_maximum_fusion.3.refs_2_), channel_id=1, source_target_pairs={{252,0},{253,1},{254,2},{255,3},{0,4},{1,5},{2,6},{3,7},{4,8},{5,9... | collective-permute-start | bytes 103688 | tf_op jit(solution)/shard_map/while/body/eval_jaxpr/ppermute | solution.py:389
  279.5 59.5 %collective-permute-start.14 = (f32[64,135]{1,0:T(8,128)S(1)}, f32[64,135]{1,0:T(8,128)S(1)}, u32[]{:S(2)}, u32[]{:S(2)}) collective-permute-start(f32[64,135]{1,0:T(8,128)S(1)} %pad_maximum_fusion.3.refs_2_), channel_id=1, source_target_pairs={{248,0},{249,1},{250,2},{251,3},{252,4},{253,5},{254,6},{255,7},{0... | collective-permute-start | bytes 103688 | tf_op jit(solution)/shard_map/while/body/eval_jaxpr/ppermute | solution.py:389
  350.3 9.5 %collective-permute-start.4 = (f32[16,135]{1,0:T(8,128)S(1)}, f32[16,135]{1,0:T(8,128)S(1)}, u32[]{:S(2)}, u32[]{:S(2)}) collective-permute-start(f32[16,135]{1,0:T(8,128)S(1)} %get-tuple-element.370.refs_4_), channel_id=1, source_target_pairs={{1,0},{2,1},{3,2},{0,3},{5,4},{6,5},{7,6},{4,7},{9,8},{10,9},{11,1... | collective-permute-start | bytes 25928 | tf_op jit(solution)/shard_map/while/body/eval_jaxpr/ppermute | solution.py:389
  351.8 8.2 collective-permute-start.3
  351.8 8.3 collective-permute-start.2
  377.3 60.7 %collective-permute-start.17 = (f32[64,135]{1,0:T(8,128)S(1)}, f32[64,135]{1,0:T(8,128)S(1)}, u32[]{:S(2)}, u32[]{:S(2)}) collective-permute-start(f32[64,135]{1,0:T(8,128)S(1)} %pad_maximum_fusion.3.refs_2_), channel_id=1, source_target_pairs={{8,0},{9,1},{10,2},{11,3},{12,4},{13,5},{14,6},{15,7},{16,8},{17,9... | collective-permute-start | bytes 103688 | tf_op jit(solution)/shard_map/while/body/eval_jaxpr/ppermute | solution.py:389
  377.3 60.6 %collective-permute-start.16 = (f32[64,135]{1,0:T(8,128)S(1)}, f32[64,135]{1,0:T(8,128)S(1)}, u32[]{:S(2)}, u32[]{:S(2)}) collective-permute-start(f32[64,135]{1,0:T(8,128)S(1)} %pad_maximum_fusion.3.refs_2_), channel_id=1, source_target_pairs={{4,0},{5,1},{6,2},{7,3},{8,4},{9,5},{10,6},{11,7},{12,8},{13,9},{1... | collective-permute-start | bytes 103688 | tf_op jit(solution)/shard_map/while/body/eval_jaxpr/ppermute | solution.py:389
  377.4 60.5 %collective-permute-start.15 = (f32[64,135]{1,0:T(8,128)S(1)}, f32[64,135]{1,0:T(8,128)S(1)}, u32[]{:S(2)}, u32[]{:S(2)}) collective-permute-start(f32[64,135]{1,0:T(8,128)S(1)} %pad_maximum_fusion.3.refs_2_), channel_id=1, source_target_pairs={{252,0},{253,1},{254,2},{255,3},{0,4},{1,5},{2,6},{3,7},{4,8},{5,9... | collective-permute-start | bytes 103688 | tf_op jit(solution)/shard_map/while/body/eval_jaxpr/ppermute | solution.py:389
  378.0 60.0 %collective-permute-start.14 = (f32[64,135]{1,0:T(8,128)S(1)}, f32[64,135]{1,0:T(8,128)S(1)}, u32[]{:S(2)}, u32[]{:S(2)}) collective-permute-start(f32[64,135]{1,0:T(8,128)S(1)} %pad_maximum_fusion.3.refs_2_), channel_id=1, source_target_pairs={{248,0},{249,1},{250,2},{251,3},{252,4},{253,5},{254,6},{255,7},{0... | collective-permute-start | bytes 103688 | tf_op jit(solution)/shard_map/while/body/eval_jaxpr/ppermute | solution.py:389
  447.6 8.3 collective-permute-start.5
  449.4 9.4 %collective-permute-start.4 = (f32[16,135]{1,0:T(8,128)S(1)}, f32[16,135]{1,0:T(8,128)S(1)}, u32[]{:S(2)}, u32[]{:S(2)}) collective-permute-start(f32[16,135]{1,0:T(8,128)S(1)} %get-tuple-element.370.refs_4_), channel_id=1, source_target_pairs={{1,0},{2,1},{3,2},{0,3},{5,4},{6,5},{7,6},{4,7},{9,8},{10,9},{11,1... | collective-permute-start | bytes 25928 | tf_op jit(solution)/shard_map/while/body/eval_jaxpr/ppermute | solution.py:389
  450.8 8.1 collective-permute-start.3
  450.8 8.1 collective-permute-start.2
  476.1 60.0 %collective-permute-start.17 = (f32[64,135]{1,0:T(8,128)S(1)}, f32[64,135]{1,0:T(8,128)S(1)}, u32[]{:S(2)}, u32[]{:S(2)}) collective-permute-start(f32[64,135]{1,0:T(8,128)S(1)} %pad_maximum_fusion.3.refs_2_), channel_id=1, source_target_pairs={{8,0},{9,1},{10,2},{11,3},{12,4},{13,5},{14,6},{15,7},{16,8},{17,9... | collective-permute-start | bytes 103688 | tf_op jit(solution)/shard_map/while/body/eval_jaxpr/ppermute | solution.py:389
  476.2 60.0 %collective-permute-start.16 = (f32[64,135]{1,0:T(8,128)S(1)}, f32[64,135]{1,0:T(8,128)S(1)}, u32[]{:S(2)}, u32[]{:S(2)}) collective-permute-start(f32[64,135]{1,0:T(8,128)S(1)} %pad_maximum_fusion.3.refs_2_), channel_id=1, source_target_pairs={{4,0},{5,1},{6,2},{7,3},{8,4},{9,5},{10,6},{11,7},{12,8},{13,9},{1... | collective-permute-start | bytes 103688 | tf_op jit(solution)/shard_map/while/body/eval_jaxpr/ppermute | solution.py:389
  476.4 59.8 %collective-permute-start.15 = (f32[64,135]{1,0:T(8,128)S(1)}, f32[64,135]{1,0:T(8,128)S(1)}, u32[]{:S(2)}, u32[]{:S(2)}) collective-permute-start(f32[64,135]{1,0:T(8,128)S(1)} %pad_maximum_fusion.3.refs_2_), channel_id=1, source_target_pairs={{252,0},{253,1},{254,2},{255,3},{0,4},{1,5},{2,6},{3,7},{4,8},{5,9... | collective-permute-start | bytes 103688 | tf_op jit(solution)/shard_map/while/body/eval_jaxpr/ppermute | solution.py:389
  476.9 59.3 %collective-permute-start.14 = (f32[64,135]{1,0:T(8,128)S(1)}, f32[64,135]{1,0:T(8,128)S(1)}, u32[]{:S(2)}, u32[]{:S(2)}) collective-permute-start(f32[64,135]{1,0:T(8,128)S(1)} %pad_maximum_fusion.3.refs_2_), channel_id=1, source_target_pairs={{248,0},{249,1},{250,2},{251,3},{252,4},{253,5},{254,6},{255,7},{0... | collective-permute-start | bytes 103688 | tf_op jit(solution)/shard_map/while/body/eval_jaxpr/ppermute | solution.py:389
  545.7 8.4 collective-permute-start.5
  547.6 9.4 %collective-permute-start.4 = (f32[16,135]{1,0:T(8,128)S(1)}, f32[16,135]{1,0:T(8,128)S(1)}, u32[]{:S(2)}, u32[]{:S(2)}) collective-permute-start(f32[16,135]{1,0:T(8,128)S(1)} %get-tuple-element.370.refs_4_), channel_id=1, source_target_pairs={{1,0},{2,1},{3,2},{0,3},{5,4},{6,5},{7,6},{4,7},{9,8},{10,9},{11,1... | collective-permute-start | bytes 25928 | tf_op jit(solution)/shard_map/while/body/eval_jaxpr/ppermute | solution.py:389
  549.0 8.1 collective-permute-start.3
  549.0 8.2 collective-permute-start.2
  574.4 60.7 %collective-permute-start.17 = (f32[64,135]{1,0:T(8,128)S(1)}, f32[64,135]{1,0:T(8,128)S(1)}, u32[]{:S(2)}, u32[]{:S(2)}) collective-permute-start(f32[64,135]{1,0:T(8,128)S(1)} %pad_maximum_fusion.3.refs_2_), channel_id=1, source_target_pairs={{8,0},{9,1},{10,2},{11,3},{12,4},{13,5},{14,6},{15,7},{16,8},{17,9... | collective-permute-start | bytes 103688 | tf_op jit(solution)/shard_map/while/body/eval_jaxpr/ppermute | solution.py:389
  574.5 60.6 %collective-permute-start.16 = (f32[64,135]{1,0:T(8,128)S(1)}, f32[64,135]{1,0:T(8,128)S(1)}, u32[]{:S(2)}, u32[]{:S(2)}) collective-permute-start(f32[64,135]{1,0:T(8,128)S(1)} %pad_maximum_fusion.3.refs_2_), channel_id=1, source_target_pairs={{4,0},{5,1},{6,2},{7,3},{8,4},{9,5},{10,6},{11,7},{12,8},{13,9},{1... | collective-permute-start | bytes 103688 | tf_op jit(solution)/shard_map/while/body/eval_jaxpr/ppermute | solution.py:389
  574.6 60.5 %collective-permute-start.15 = (f32[64,135]{1,0:T(8,128)S(1)}, f32[64,135]{1,0:T(8,128)S(1)}, u32[]{:S(2)}, u32[]{:S(2)}) collective-permute-start(f32[64,135]{1,0:T(8,128)S(1)} %pad_maximum_fusion.3.refs_2_), channel_id=1, source_target_pairs={{252,0},{253,1},{254,2},{255,3},{0,4},{1,5},{2,6},{3,7},{4,8},{5,9... | collective-permute-start | bytes 103688 | tf_op jit(solution)/shard_map/while/body/eval_jaxpr/ppermute | solution.py:389
  575.1 60.0 %collective-permute-start.14 = (f32[64,135]{1,0:T(8,128)S(1)}, f32[64,135]{1,0:T(8,128)S(1)}, u32[]{:S(2)}, u32[]{:S(2)}) collective-permute-start(f32[64,135]{1,0:T(8,128)S(1)} %pad_maximum_fusion.3.refs_2_), channel_id=1, source_target_pairs={{248,0},{249,1},{250,2},{251,3},{252,4},{253,5},{254,6},{255,7},{0... | collective-permute-start | bytes 103688 | tf_op jit(solution)/shard_map/while/body/eval_jaxpr/ppermute | solution.py:389
  644.7 8.3 collective-permute-start.5
  646.5 9.4 %collective-permute-start.4 = (f32[16,135]{1,0:T(8,128)S(1)}, f32[16,135]{1,0:T(8,128)S(1)}, u32[]{:S(2)}, u32[]{:S(2)}) collective-permute-start(f32[16,135]{1,0:T(8,128)S(1)} %get-tuple-element.370.refs_4_), channel_id=1, source_target_pairs={{1,0},{2,1},{3,2},{0,3},{5,4},{6,5},{7,6},{4,7},{9,8},{10,9},{11,1... | collective-permute-start | bytes 25928 | tf_op jit(solution)/shard_map/while/body/eval_jaxpr/ppermute | solution.py:389
  647.9 8.1 collective-permute-start.3
  647.9 8.1 collective-permute-start.2
  673.3 60.3 %collective-permute-start.17 = (f32[64,135]{1,0:T(8,128)S(1)}, f32[64,135]{1,0:T(8,128)S(1)}, u32[]{:S(2)}, u32[]{:S(2)}) collective-permute-start(f32[64,135]{1,0:T(8,128)S(1)} %pad_maximum_fusion.3.refs_2_), channel_id=1, source_target_pairs={{8,0},{9,1},{10,2},{11,3},{12,4},{13,5},{14,6},{15,7},{16,8},{17,9... | collective-permute-start | bytes 103688 | tf_op jit(solution)/shard_map/while/body/eval_jaxpr/ppermute | solution.py:389
  673.3 60.2 %collective-permute-start.16 = (f32[64,135]{1,0:T(8,128)S(1)}, f32[64,135]{1,0:T(8,128)S(1)}, u32[]{:S(2)}, u32[]{:S(2)}) collective-permute-start(f32[64,135]{1,0:T(8,128)S(1)} %pad_maximum_fusion.3.refs_2_), channel_id=1, source_target_pairs={{4,0},{5,1},{6,2},{7,3},{8,4},{9,5},{10,6},{11,7},{12,8},{13,9},{1... | collective-permute-start | bytes 103688 | tf_op jit(solution)/shard_map/while/body/eval_jaxpr/ppermute | solution.py:389
  673.5 60.0 %collective-permute-start.15 = (f32[64,135]{1,0:T(8,128)S(1)}, f32[64,135]{1,0:T(8,128)S(1)}, u32[]{:S(2)}, u32[]{:S(2)}) collective-permute-start(f32[64,135]{1,0:T(8,128)S(1)} %pad_maximum_fusion.3.refs_2_), channel_id=1, source_target_pairs={{252,0},{253,1},{254,2},{255,3},{0,4},{1,5},{2,6},{3,7},{4,8},{5,9... | collective-permute-start | bytes 103688 | tf_op jit(solution)/shard_map/while/body/eval_jaxpr/ppermute | solution.py:389
  674.0 59.6 %collective-permute-start.14 = (f32[64,135]{1,0:T(8,128)S(1)}, f32[64,135]{1,0:T(8,128)S(1)}, u32[]{:S(2)}, u32[]{:S(2)}) collective-permute-start(f32[64,135]{1,0:T(8,128)S(1)} %pad_maximum_fusion.3.refs_2_), channel_id=1, source_target_pairs={{248,0},{249,1},{250,2},{251,3},{252,4},{253,5},{254,6},{255,7},{0... | collective-permute-start | bytes 103688 | tf_op jit(solution)/shard_map/while/body/eval_jaxpr/ppermute | solution.py:389
  743.2 8.3 collective-permute-start.5
  745.0 9.4 %collective-permute-start.4 = (f32[16,135]{1,0:T(8,128)S(1)}, f32[16,135]{1,0:T(8,128)S(1)}, u32[]{:S(2)}, u32[]{:S(2)}) collective-permute-start(f32[16,135]{1,0:T(8,128)S(1)} %get-tuple-element.370.refs_4_), channel_id=1, source_target_pairs={{1,0},{2,1},{3,2},{0,3},{5,4},{6,5},{7,6},{4,7},{9,8},{10,9},{11,1... | collective-permute-start | bytes 25928 | tf_op jit(solution)/shard_map/while/body/eval_jaxpr/ppermute | solution.py:389
  746.4 8.1 collective-permute-start.3
  746.4 8.1 collective-permute-start.2
  771.7 60.5 %collective-permute-start.17 = (f32[64,135]{1,0:T(8,128)S(1)}, f32[64,135]{1,0:T(8,128)S(1)}, u32[]{:S(2)}, u32[]{:S(2)}) collective-permute-start(f32[64,135]{1,0:T(8,128)S(1)} %pad_maximum_fusion.3.refs_2_), channel_id=1, source_target_pairs={{8,0},{9,1},{10,2},{11,3},{12,4},{13,5},{14,6},{15,7},{16,8},{17,9... | collective-permute-start | bytes 103688 | tf_op jit(solution)/shard_map/while/body/eval_jaxpr/ppermute | solution.py:389
  771.8 60.4 %collective-permute-start.16 = (f32[64,135]{1,0:T(8,128)S(1)}, f32[64,135]{1,0:T(8,128)S(1)}, u32[]{:S(2)}, u32[]{:S(2)}) collective-permute-start(f32[64,135]{1,0:T(8,128)S(1)} %pad_maximum_fusion.3.refs_2_), channel_id=1, source_target_pairs={{4,0},{5,1},{6,2},{7,3},{8,4},{9,5},{10,6},{11,7},{12,8},{13,9},{1... | collective-permute-start | bytes 103688 | tf_op jit(solution)/shard_map/while/body/eval_jaxpr/ppermute | solution.py:389
  772.0 60.2 %collective-permute-start.15 = (f32[64,135]{1,0:T(8,128)S(1)}, f32[64,135]{1,0:T(8,128)S(1)}, u32[]{:S(2)}, u32[]{:S(2)}) collective-permute-start(f32[64,135]{1,0:T(8,128)S(1)} %pad_maximum_fusion.3.refs_2_), channel_id=1, source_target_pairs={{252,0},{253,1},{254,2},{255,3},{0,4},{1,5},{2,6},{3,7},{4,8},{5,9... | collective-permute-start | bytes 103688 | tf_op jit(solution)/shard_map/while/body/eval_jaxpr/ppermute | solution.py:389
  772.5 59.8 %collective-permute-start.14 = (f32[64,135]{1,0:T(8,128)S(1)}, f32[64,135]{1,0:T(8,128)S(1)}, u32[]{:S(2)}, u32[]{:S(2)}) collective-permute-start(f32[64,135]{1,0:T(8,128)S(1)} %pad_maximum_fusion.3.refs_2_), channel_id=1, source_target_pairs={{248,0},{249,1},{250,2},{251,3},{252,4},{253,5},{254,6},{255,7},{0... | collective-permute-start | bytes 103688 | tf_op jit(solution)/shard_map/while/body/eval_jaxpr/ppermute | solution.py:389
  (141 other events, 690.8 us)
where the time goes:
time: 912 us; the launch traced here: 898 us
  blocking collectives  395 us (43%)
  starting transfers between devices  240 us (26%)
  waiting for transfers between devices  98.4 us (11%)
  local copies, waits for them, and re-layouts  76.5 us (8%)
  Pallas kernels  71.1 us (8%)
  loops' own time  11.6 us (1%)
    all_gather x7, blocking collectives, gathered(): return lax.all_gather(part, ('dom', 'blk'), axis=0, tiled=True)  395 us
    ppermute x144, starting transfers between devices, shifted(): return lax.ppermute(array, ('dom', 'blk'), pairs)  187 us
    pallas_call x22, Pallas kernels, call(): pl.pallas_call(body, out_shape=out_shape, in_specs=specs if specs is not...  71.1 us
    ppermute x144, waiting for transfers between devices, shifted(): return lax.ppermute(array, ('dom', 'blk'), pairs)  64.3 us
    ppermute x36, starting transfers between devices, added(): lax.ppermute(part, ('dom', 'blk'), [(n ^ k * reach, n) for n in range(dev...  53.3 us
    while x70, local copies, waits for them, and re-layouts  47.3 us
    ppermute x36, waiting for transfers between devices, added(): lax.ppermute(part, ('dom', 'blk'), [(n ^ k * reach, n) for n in range(dev...  34.1 us
    unnamed x24, local copies, waits for them, and re-layouts  20.1 us
  transfers between devices with their start and end apart: 180, of which 66 were waited for; matrix products, arithmetic and copies ran while one was open for 1% of the time, Pallas kernels for 5%

commit v1 on v0

--- a/solution.py
+++ b/solution.py
@@ -9,6 +9,8 @@
 
 STEPS = 8
 EPS = 1e-06
+KEPT = 2e-3
+SAMPLE = 16
 LANES = 128
 ROWS = 136
 INTERPRET = False
@@ -25,6 +27,10 @@
 
 def in_vmem(array):
     return array if INTERPRET else pltpu.with_memory_space_constraint(array, pltpu.VMEM)
+
+
+def in_hbm(array):
+    return array if INTERPRET else pltpu.with_memory_space_constraint(array, pltpu.HBM)
 
 
 def call(body, out_shape, *args, scratch=(), limit=24, specs=None):
@@ -63,16 +69,17 @@
     return dot(lh, rh) + (dot(lh, rl) + dot(ll, rh))
 
 
-def pack_body(jac_hbm, main_ref, rest_ref):
+def pack_body(jac_hbm, main_ref, rest_ref, token_ref):
     faces, rows, elems, cols = jac_hbm.shape
-    chunk = 27
+    chunk, group = 27, 9
+    token_ref[...] = jnp.zeros(token_ref.shape, f32)
     extra = cols - LANES
 
     def step(block, at=None):
         at = (pl.program_id(0) if at is None else at) * chunk
         lane = lax.broadcasted_iota(jnp.int32, (elems, LANES), 1)
 
-        def row(i, _):
+        def row(i):
             packed = jnp.zeros((elems, LANES), f32)
             for f in range(faces):
                 main_ref[f, at + i] = block[f, i, :, 0:LANES]
@@ -83,9 +90,13 @@
                     tail = pltpu.roll(tail, f * extra, 1)
                 packed = packed + tail
             rest_ref[at + i] = packed
+
+        def some(g, _):
+            for n in range(group):
+                row(g * group + n)
             return 0
 
-        lax.fori_loop(0, chunk, row, 0)
+        lax.fori_loop(0, chunk // group, some, 0)
 
     if INTERPRET:
         for c in range(rows // chunk):
@@ -98,72 +109,62 @@
     )(jac_hbm)
 
 
-def invert_body(pivot_ref, lower_ref, upper_ref, main_ref, rest_ref, part_ref, wide_ref, side_ref):
-    lines, levels, height, _ = main_ref.shape
+def invert_body(l, lines, pivot_ref, lower_ref, upper_ref, main_ref, rest_ref, token_ref, part_ref, wide_ref, side_ref):
+    levels, height, _ = main_ref.shape
     cols = part_ref.shape[2]
     extra = cols - LANES
     rows_by_rows = ((1,), (1,))
     rows_by_cols = ((1,), (0,))
-    pivot_rows, pair_rows = levels * cols, lines * cols
-
-    def line(l, _):
-        wide_ref[0:pivot_rows, :] = pivot_ref[l, :, 0:LANES]
-        side_ref[0:pivot_rows, 0:extra] = pivot_ref[l, :, LANES:cols]
-
-        def strided(first, count):
-            at = pl.ds(first, cols, stride=count)
-            return jnp.concatenate([wide_ref[at, :], side_ref[at, :][:, 0:extra]], 1)
-
-        def pivot_of(k):
-            return strided(k, levels)
-
-        def paired(ref, k):
-            wide_ref[pivot_rows:, :] = ref[k, :, 0:LANES]
-            side_ref[pivot_rows:, 0:extra] = ref[k, :, LANES:cols]
-            return strided(pivot_rows + l, lines)
-
-        part_ref[...] = jnp.zeros(part_ref.shape, f32)
-        part_ref[0, 0:cols, :] = pivot_of(0).T
-
-        def forward(k, _):
-            pivot = pivot_of(k)
-            mixed = product(pivot, paired(lower_ref, k - 1), rows_by_cols)
-            part_ref[k] = -product(part_ref[k - 1], mixed, rows_by_rows)
-            part_ref[k, pl.ds(pl.multiple_of(k * ROWS, 8), cols), :] = pivot.T
-            return 0
-
-        lax.fori_loop(1, levels, forward, 0)
-
-        def backward(i, _):
-            k = levels - 2 - i
-            part_ref[k] = part_ref[k] - product(
-                part_ref[k + 1], paired(upper_ref, k), rows_by_rows
+    pivot_rows = levels * cols
+    token_ref[...] = jnp.zeros(token_ref.shape, f32)
+    wide_ref[0:pivot_rows, :] = pivot_ref[l, :, 0:LANES]
+    side_ref[0:pivot_rows, 0:extra] = pivot_ref[l, :, LANES:cols]
+
+    def strided(first, count):
+        at = pl.ds(first, cols, stride=count)
+        return jnp.concatenate([wide_ref[at, :], side_ref[at, :][:, 0:extra]], 1)
+
+    def paired(ref, k):
+        wide_ref[pivot_rows:, :] = ref[k, :, 0:LANES]
+        side_ref[pivot_rows:, 0:extra] = ref[k, :, LANES:cols]
+        return strided(pivot_rows + l, lines)
+
+    part_ref[...] = jnp.zeros(part_ref.shape, f32)
+    part_ref[0, 0:cols, :] = strided(0, levels).T
+    for k in range(1, levels):
+        pivot = strided(k, levels)
+        mixed = product(pivot, paired(lower_ref, k - 1), rows_by_cols)
+        before = part_ref[k - 1, 0 : k * ROWS, :]
+        part_ref[k, 0 : k * ROWS, :] = -product(before, mixed, rows_by_rows)
+        part_ref[k, k * ROWS : k * ROWS + cols, :] = pivot.T
+
+    def backward(i, _):
+        k = levels - 2 - i
+        part_ref[k] = part_ref[k] - product(part_ref[k + 1], paired(upper_ref, k), rows_by_rows)
+        return 0
+
+    lax.fori_loop(0, levels - 1, backward, 0)
+
+    def emit(t, _):
+        at = pl.ds(pl.multiple_of(t * ROWS, 8), ROWS)
+        packed = jnp.zeros((ROWS, LANES), f32)
+        for k in range(levels):
+            main_ref[k, at, :] = part_ref[k, at, 0:LANES]
+            tail = jnp.concatenate(
+                [part_ref[k, at, LANES:cols], jnp.zeros((ROWS, LANES - extra), f32)], 1
             )
-            return 0
-
-        lax.fori_loop(0, levels - 1, backward, 0)
-
-        def emit(t, _):
-            at = pl.ds(pl.multiple_of(t * ROWS, 8), ROWS)
-            packed = jnp.zeros((ROWS, LANES), f32)
-            for k in range(levels):
-                main_ref[l, k, at, :] = part_ref[k, at, 0:LANES]
-                tail = jnp.concatenate(
-                    [part_ref[k, at, LANES:cols], jnp.zeros((ROWS, LANES - extra), f32)], 1
-                )
-                packed = packed + (pltpu.roll(tail, k * extra, 1) if k else tail)
-            rest_ref[l, at, :] = packed
-            return 0
-
-        lax.fori_loop(0, levels, emit, 0)
+            packed = packed + (pltpu.roll(tail, k * extra, 1) if k else tail)
+        rest_ref[at, :] = packed
         return 0
 
-    lax.fori_loop(0, lines, line, 0)
-
-
-def solve_body(*refs):
-    *blocks, hits_ref, main_ref, rest_ref, out_ref, pool_ref, wide_ref = refs
-    lines, levels, height, _ = main_ref.shape
+    lax.fori_loop(0, levels, emit, 0)
+
+
+def solve_body(lines, *refs):
+    blocks, refs = refs[: -4 - 2 * lines], refs[-4 - 2 * lines :]
+    hits_ref, out_ref, pool_ref, wide_ref = refs[0], *refs[-3:]
+    mains, rests = refs[1 : 1 + lines], refs[1 + lines : 1 + 2 * lines]
+    levels = mains[0].shape[0]
     count = hits_ref.shape[0]
     cols = pool_ref.shape[1]
     extra = cols - LANES
@@ -181,8 +182,8 @@
                 at = pl.ds(pl.multiple_of(m * ROWS + t * 8, 8), 8)
                 value = wide_ref[l * levels + m, t * 8 : t * 8 + 8, :]
                 for k in range(levels):
-                    sums[k] = sums[k] + main_ref[l, k, at, :] * value
-                sums[levels] = sums[levels] + rest_ref[l, at, :] * value
+                    sums[k] = sums[k] + mains[l][k, at, :] * value
+                sums[levels] = sums[levels] + rests[l][at, :] * value
             return tuple(sums)
 
         zero = jnp.zeros((8, LANES), f32)
@@ -261,9 +262,22 @@
     return jnp.sum(parts_ref[...], axis=0, keepdims=True)
 
 
-def project_body(images_ref, residual_ref, out_ref):
+def project_body(images_ref, residual_ref, jac_ref, pivot_ref, out_ref):
     residual = residual_ref[...]
-    out_ref[...] = row_of({k: images_ref[k] * residual for k in range(images_ref.shape[0])})
+    products = {k: images_ref[k] * residual for k in range(STEPS)}
+    lane = lax.broadcasted_iota(jnp.int32, jac_ref.shape[1:], 1)
+    own = jnp.zeros(jac_ref.shape[1:], f32)
+    for i in range(SAMPLE):
+        own = jnp.where(lane == i, jac_ref[i], own)
+    products[STEPS] = own
+    lines, _, levels, _ = pivot_ref.shape
+    lane = lax.broadcasted_iota(jnp.int32, pivot_ref.shape[2:], 1)
+    own = jnp.zeros(pivot_ref.shape[2:], f32)
+    for l in range(lines):
+        for i in range(SAMPLE):
+            own = own + jnp.where(lane == i, pivot_ref[l, i], 0.0)
+    products[STEPS + 1] = own
+    out_ref[...] = row_of(products)
 
 
 def deflate_body(entries, parts_ref, residual_ref, basis_ref, images_ref, correction_ref, start_ref):
@@ -276,6 +290,81 @@
         start = start - weight * images_ref[k]
     correction_ref[...] = correction
     start_ref[...] = start
+
+
+def shift_of(row, count):
+    return lane_of(row, STEPS) / count * (lane_of(row, STEPS + 1) / count)
+
+
+def power_body(count, *refs):
+    *blocks, u_ref, row_ref, hits_ref, main_ref, rest_ref, out_ref, pool_ref = refs
+    image = operate(blocks, hits_ref, main_ref, rest_ref, pool_ref)
+    out_ref[...] = image - shift_of(row_ref[...], count) * u_ref[...]
+
+
+def power_last_body(count, *refs):
+    blocks, vectors, refs = refs[: -8 - STEPS], refs[-8 - STEPS : -8], refs[-8:]
+    u_ref, row_ref, hits_ref, main_ref, rest_ref, out_ref, part_ref, pool_ref = refs
+    image = operate(blocks, hits_ref, main_ref, rest_ref, pool_ref)
+    last = image - shift_of(row_ref[...], count) * u_ref[...]
+    out_ref[...] = last
+    vectors = [v[...] for v in vectors] + [last]
+    at = lax.broadcasted_iota(jnp.int32, part_ref.shape, 0)
+    lane = lax.broadcasted_iota(jnp.int32, part_ref.shape, 1)
+    part = jnp.zeros(part_ref.shape, f32)
+    for k, right in enumerate(vectors):
+        for i in range(k + 1):
+            total = jnp.sum(vectors[i] * right, axis=0, keepdims=True)
+            total = jnp.sum(total, axis=1, keepdims=True)
+            here = ((at == i) & (lane == k)) | ((at == k) & (lane == i))
+            part = jnp.where(here, total, part)
+    part_ref[...] = part
+
+
+def combine_body(entries, count, *refs):
+    gram_ref, row_ref, *vectors = refs[: 3 + STEPS]
+    basis_out, hess_out, norm_ref, sure_ref = refs[3 + STEPS :]
+    shift = shift_of(row_ref[...], count)
+    gram = gram_ref[...] / entries
+    size = jnp.abs(gram)
+    at = lax.broadcasted_iota(jnp.int32, gram.shape, 0)
+    lane = lax.broadcasted_iota(jnp.int32, gram.shape, 1)
+
+    def across(values):
+        return jnp.sum(values, axis=1, keepdims=True)
+
+    def turned(column):
+        return jnp.sum(jnp.where(at == lane, column, 0.0), axis=0, keepdims=True)
+
+    def times(matrix, row):
+        return turned(across(matrix * row))
+
+    first = lane[0:1]
+    norm = jnp.sqrt(gram[0:1, 0:1] + EPS)
+    norm_ref[...] = jnp.broadcast_to(norm, (1, LANES))
+    newest = jnp.where(first == 0, 1.0 / norm, 0.0)
+    known = jnp.where(at == 0, newest, 0.0)
+    sure = jnp.full((1, 1), 1.0, f32)
+    for j in range(STEPS):
+        moved = pltpu.roll(jnp.broadcast_to(newest, (8, LANES)), 1, 1)[0:1]
+        image = moved + shift * newest
+        inner = across(known * times(gram, image))
+        reduced = image - jnp.sum(known * inner, axis=0, keepdims=True)
+        square = across(reduced * times(gram, reduced))
+        terms = across(jnp.abs(reduced) * times(size, jnp.abs(reduced)))
+        sure = jnp.where(square > KEPT * terms, sure, 0.0)
+        below = jnp.sqrt(jnp.maximum(square, 0.0) + EPS)
+        column = jnp.where(first <= j, turned(inner), 0.0)
+        hess_out[j : j + 1, :] = jnp.where(first == j + 1, below, column)
+        newest = reduced / below
+        known = jnp.where(at == j + 1, newest, known)
+    sure_ref[...] = jnp.broadcast_to(sure, (1, LANES))
+    vectors = [v[...] for v in vectors]
+    for j in range(STEPS + 1):
+        value = known[j : j + 1, 0:1] * vectors[0]
+        for k in range(1, j + 1):
+            value = value + known[j : j + 1, k : k + 1] * vectors[k]
+        basis_out[j] = value
 
 
 def first_body(*refs):
@@ -389,25 +478,14 @@
     return lax.ppermute(array, ("dom", "blk"), pairs)
 
 
-def partition(array):
-    return [shifted(array, 0, b) for b in range(lax.axis_size("blk"))]
-
-
-def near_rows(array):
+def around(array, reach):
     blks = lax.axis_size("blk")
-    return [shifted(array, d, b) for d in (-1, 0, 1) for b in range(blks)]
-
-
-def far_rows(array):
-    whole = jnp.concatenate(partition(array), 0)
-    return [shifted(whole, d, 0) for d in (-2, -1, 0, 1, 2)]
-
-
-def gathered(part):
-    return lax.all_gather(part, ("dom", "blk"), axis=0, tiled=True)
-
-
-def added(part):
+    whole = jnp.concatenate([shifted(array, 0, b) for b in range(blks)], 0)
+    return [shifted(whole, d, 0) for d in range(-reach, reach + 1)]
+
+
+def added(part, beside=()):
+    beside = list(beside)
     doms, blks = lax.axis_size("dom"), lax.axis_size("blk")
     devices = doms * blks
     reach = 1
@@ -421,23 +499,65 @@
             part = (part + others[0]) + (others[1] + others[2])
         else:
             part = part + others[0]
+        if beside:
+            part = part + beside.pop(0)()
         reach *= ways
     return part
+
+
+def matrices_of(jacobian, line_pivots, line_lower, line_upper):
+    elems, faces, cols, _ = jacobian.shape
+    lines, levels = line_pivots.shape[:2]
+    height = levels * ROWS
+    token = jax.ShapeDtypeStruct((1, LANES), f32)
+    kept = {}
+
+    def pack():
+        main, rest, done = call(
+            pack_body,
+            [vmem_out((faces, cols, elems, LANES)), vmem_out((cols, elems, LANES)), token],
+            in_hbm(jnp.transpose(jacobian, (1, 2, 0, 3))),
+            specs=[pl.BlockSpec(memory_space=pltpu.VMEM if INTERPRET else pltpu.HBM)],
+            limit=16,
+        )
+        kept["jac"] = in_vmem(main), in_vmem(rest)
+        return done
+
+    pivots = jnp.transpose(line_pivots, (0, 2, 1, 3)).reshape(lines, cols * levels, cols)
+    lower = jnp.transpose(line_lower, (1, 2, 0, 3)).reshape(levels - 1, cols * lines, cols)
+    upper = jnp.transpose(line_upper, (1, 2, 0, 3)).reshape(levels - 1, cols * lines, cols)
+
+    def invert(l):
+        main, rest, done = call(
+            functools.partial(invert_body, l, lines),
+            [vmem_out((levels, height, LANES)), vmem_out((height, LANES)), token],
+            pivots,
+            lower,
+            upper,
+            scratch=[
+                pltpu.VMEM((levels, height, cols), f32),
+                pltpu.VMEM(((levels + lines) * cols, LANES), f32),
+                pltpu.VMEM(((levels + lines) * cols, LANES), f32),
+            ],
+            limit=32,
+        )
+        kept[l] = in_vmem(main), in_vmem(rest)
+        return done
+
+    return [functools.partial(invert, l) for l in range(lines)] + [pack], kept
 
 
 def per_device(residual, recycle_basis, recycle_images, jacobian, neighbours, line_members,
                line_pivots, line_lower, line_upper):
     elems, cols = residual.shape
     doms, blks = lax.axis_size("dom"), lax.axis_size("blk")
-    faces = jacobian.shape[1]
     lines, levels = line_pivots.shape[:2]
     entries = float(elems * cols * doms * blks)
+    count = float(elems * SAMPLE * doms * blks)
     dom, blk = lax.axis_index("dom"), lax.axis_index("blk")
     devices = doms * blks
-
     row = jax.ShapeDtypeStruct((1, LANES), f32)
     rows = jax.ShapeDtypeStruct((elems, cols), f32)
-    projected = added(call(project_body, row, recycle_images, residual))
 
     members = line_members.reshape(devices, elems)
     near = jnp.array([(d, b) for d in range(-2, 3) for b in range(blks)], jnp.int32)
@@ -451,37 +571,14 @@
     stencil = (wanted[:, None] == line_ids[None, :]).astype(f32)
     mine = lax.dynamic_slice_in_dim(members, me, 1, 0)[0]
     entering = (mine[:, None] == elem_ids[None, :]).astype(f32)
-
-    spec = pl.BlockSpec(memory_space=pltpu.VMEM)
-    hbm = pl.BlockSpec(memory_space=pl.ANY)
-    jac = jnp.transpose(jacobian, (1, 2, 0, 3))
-    jac_main, jac_rest = call(
-        pack_body,
-        [vmem_out((faces, cols, elems, LANES)), vmem_out((cols, elems, LANES))],
-        jac,
-        specs=[spec if INTERPRET else hbm],
-        limit=24,
-    )
-    pivots = jnp.transpose(line_pivots, (0, 2, 1, 3)).reshape(lines, cols * levels, cols)
-    lower = jnp.transpose(line_lower, (1, 2, 0, 3)).reshape(levels - 1, cols * lines, cols)
-    upper = jnp.transpose(line_upper, (1, 2, 0, 3)).reshape(levels - 1, cols * lines, cols)
-    height = levels * ROWS
-    inv_main, inv_rest = call(
-        invert_body,
-        [vmem_out((lines, levels, height, LANES)), vmem_out((lines, height, LANES))],
-        pivots,
-        lower,
-        upper,
-        scratch=[
-            pltpu.VMEM((levels, height, cols), f32),
-            pltpu.VMEM(((levels + lines) * cols, LANES), f32),
-            pltpu.VMEM(((levels + lines) * cols, LANES), f32),
-        ],
-        limit=40,
-    )
-    jac_main, jac_rest, inv_main, inv_rest = map(in_vmem, (jac_main, jac_rest, inv_main, inv_rest))
-
-    correction, u = call(
+    stencil_pool = pltpu.VMEM((stencil.shape[1], cols), f32)
+
+    sample_jac = jnp.transpose(jacobian[:, 0, :SAMPLE], (1, 0, 2))
+    sample_pivots = jnp.transpose(line_pivots[:, :, :SAMPLE], (0, 2, 1, 3))
+    part = call(project_body, row, recycle_images, residual, sample_jac, sample_pivots)
+    calls, kept = matrices_of(jacobian, line_pivots, line_lower, line_upper)
+    projected = added(part, calls)
+    correction, start = call(
         functools.partial(deflate_body, entries),
         [rows, rows],
         projected,
@@ -490,74 +587,110 @@
         recycle_images,
     )
 
-    def precondition(v):
+    def precondition(v, kept):
         z = call(
-            solve_body,
+            functools.partial(solve_body, lines),
             rows,
-            *near_rows(v),
+            *around(v, 1),
             entering,
-            inv_main,
-            inv_rest,
+            *[kept[l][0] for l in range(lines)],
+            *[kept[l][1] for l in range(lines)],
             scratch=[
                 pltpu.VMEM((entering.shape[1], cols), f32),
                 pltpu.VMEM((elems, ROWS, LANES), f32),
             ],
         )
-        return far_rows(z)
-
-    stencil_pool = pltpu.VMEM((stencil.shape[1], cols), f32)
-    matrices = (stencil, jac_main, jac_rest)
-    c, part = call(
-        first_body, [rows, row], *precondition(u), u, *matrices, scratch=[stencil_pool]
+        return around(z, 2)
+
+    vectors = [start]
+    matrix = jax.ShapeDtypeStruct((2 * STEPS, LANES), f32)
+    for j in range(STEPS):
+        last = j == STEPS - 1
+        result = call(
+            functools.partial(power_last_body if last else power_body, count),
+            [rows, matrix] if last else rows,
+            *precondition(vectors[-1], kept),
+            *(vectors if last else ()),
+            vectors[-1],
+            projected,
+            stencil,
+            *kept["jac"],
+            scratch=[stencil_pool],
+        )
+        vectors.append(result[0] if last else result)
+    gram = added(result[1])
+    small = jax.ShapeDtypeStruct((STEPS, LANES), f32)
+    stacked = jax.ShapeDtypeStruct((STEPS + 1, elems, cols), f32)
+    basis, hessenberg, norm, sure = call(
+        functools.partial(combine_body, entries, count),
+        [stacked, small, row, row],
+        gram,
+        projected,
+        *vectors,
     )
-    stack = jax.ShapeDtypeStruct((STEPS, elems, cols), f32)
-    hess = jax.ShapeDtypeStruct((2 * STEPS, LANES), f32)
-
-    def step(_, state):
-        basis, images, hessenberg, u, c, v, known, part = state
+
+    def stepwise(start):
+        calls, kept = matrices_of(jacobian, line_pivots, line_lower, line_upper)
+        for each in calls:
+            each()
+        matrices = (stencil, *kept["jac"])
+        c, part = call(
+            first_body,
+            [rows, row],
+            *precondition(start, kept),
+            start,
+            *matrices,
+            scratch=[stencil_pool],
+        )
+        stack = jax.ShapeDtypeStruct((STEPS, elems, cols), f32)
+
+        def step(_, state):
+            basis, images, hessenberg, u, c, v, known, part = state
+            return tuple(
+                call(
+                    functools.partial(next_body, entries),
+                    [stack, stack, matrix, rows, rows, rows, row, row],
+                    *precondition(v, kept),
+                    *matrices,
+                    added(part),
+                    u,
+                    c,
+                    known,
+                    basis,
+                    images,
+                    hessenberg,
+                    scratch=[stencil_pool],
+                )
+            )
+
+        empty = jnp.zeros(stack.shape, f32)
+        known = jnp.zeros((1, LANES), f32).at[0, SCALE].set(1.0)
+        state = (empty, empty, jnp.zeros(matrix.shape, f32), start, c, c, known, part)
+        basis, _, hessenberg, u, c, _, known, part = lax.fori_loop(0, STEPS - 1, step, state)
+        basis, hessenberg, u, known, part = call(
+            functools.partial(last_body, entries),
+            [stack, matrix, rows, row, row],
+            added(part),
+            u,
+            c,
+            known,
+            basis,
+            hessenberg,
+        )
         return tuple(
             call(
-                functools.partial(next_body, entries),
-                [stack, stack, hess, rows, rows, rows, row, row],
-                *precondition(v),
-                *matrices,
-                gathered(part),
+                functools.partial(finish_body, entries),
+                [stacked, small, row],
+                added(part),
                 u,
-                c,
                 known,
                 basis,
-                images,
                 hessenberg,
-                scratch=[stencil_pool],
             )
         )
 
-    empty = jnp.zeros(stack.shape, f32)
-    known = jnp.zeros((1, LANES), f32).at[0, SCALE].set(1.0)
-    state = (empty, empty, jnp.zeros(hess.shape, f32), u, c, c, known, part)
-    basis, _, hessenberg, u, c, _, known, part = lax.fori_loop(0, STEPS - 1, step, state)
-    basis, hessenberg, u, known, part = call(
-        functools.partial(last_body, entries),
-        [stack, hess, rows, row, row],
-        added(part),
-        u,
-        c,
-        known,
-        basis,
-        hessenberg,
-    )
-    basis, hessenberg, norm = call(
-        functools.partial(finish_body, entries),
-        [
-            jax.ShapeDtypeStruct((STEPS + 1, elems, cols), f32),
-            jax.ShapeDtypeStruct((STEPS, LANES), f32),
-            row,
-        ],
-        added(part),
-        u,
-        known,
-        basis,
-        hessenberg,
+    basis, hessenberg, norm = lax.cond(
+        sure[0, 0] > 0.5, lambda start: (basis, hessenberg, norm), stepwise, start
     )
     return correction, basis, hessenberg[:, : STEPS + 1].T, norm[0, 0]
 

time: 912 us -> 398 us (0.44)
  blocking collectives: 395 us -> 0 us
  starting transfers between devices: 240 us -> 153 us
  local copies, waits for them, and re-layouts: 76.5 us -> 32 us
  waiting for transfers between devices: 98.4 us -> 141 us
  Pallas kernels: 71.1 us -> 59.8 us
  loops' own time: 11.6 us -> 1.19 us
    all_gather x7 -> x0, blocking collectives: 395 us -> none  [gathered(): return lax.all_gather(part, ('dom', 'blk'), axis=0, tiled=True)]
    ppermute x144 -> x96, starting transfers between devices: 187 us -> 99.8 us  [shifted(): return lax.ppermute(array, ('dom', 'blk'), pairs)]
    ppermute x144 -> x96, waiting for transfers between devices: 64.3 us -> 124 us  [shifted(): return lax.ppermute(array, ('dom', 'blk'), pairs)]
    while x70 -> x0, local copies, waits for them, and re-layouts: 47.3 us -> none
    ppermute x36 -> x24, waiting for transfers between devices: 34.1 us -> 16.6 us  [added(): lax.ppermute(part, ('dom', 'blk'), [(n ^ k * reach, n) for n in range(dev...]
    pallas_call x22, Pallas kernels: 71.1 us -> 59.8 us  [call(): pl.pallas_call(body, out_shape=out_shape, in_specs=specs if specs is not...]
    another operation x1, loops' own time: 11.6 us -> 1.19 us  [per_device(): lax.cond(sure[0, 0] > 0.5, lambda start: (basis, hessenberg, norm), stepw...]
    unnamed x24 -> x53, local copies, waits for them, and re-layouts: 20.1 us -> 21.3 us
  transfers between devices with their start and end apart: 180 -> 120, of which waited for: 66 -> 100; matrix products, arithmetic and copies ran while one was open for 1% -> 3% of each run, Pallas kernels for 5% -> 7%
where the time goes in v1:
time: 398 us; the launch traced here: 390 us
  starting transfers between devices  153 us (38%)
  waiting for transfers between devices  141 us (35%)
  Pallas kernels  59.8 us (15%)
  local copies, waits for them, and re-layouts  32 us (8%)
    ppermute x96, waiting for transfers between devices, shifted(): return lax.ppermute(array, ('dom', 'blk'), pairs)  124 us
    ppermute x96, starting transfers between devices, shifted(): return lax.ppermute(array, ('dom', 'blk'), pairs)  99.8 us
    pallas_call x22, Pallas kernels, call(): pl.pallas_call(body, out_shape=out_shape, in_specs=specs if specs is not...  59.8 us
    ppermute x24, starting transfers between devices, added(): lax.ppermute(part, ('dom', 'blk'), [(n ^ k * reach, n) for n in range(dev...  53.3 us
    unnamed x53, local copies, waits for them, and re-layouts  21.3 us
    ppermute x24, waiting for transfers between devices, added(): lax.ppermute(part, ('dom', 'blk'), [(n ^ k * reach, n) for n in range(dev...  16.6 us
  transfers between devices with their start and end apart: 120, of which 100 were waited for; matrix products, arithmetic and copies ran while one was open for 3% of the time, Pallas kernels for 7%

profile of v1, /device:TPU:68, one launch (start us, length us, event | category | flops | bytes accessed | tf_op | source)
XLA Modules:
  0.0 389.9 jit_solution(15194725453317731206)
XLA Ops:
  4.4 3.1 collective-permute-start.62
  10.4 3.5 reshape.102.upper_ref
  13.9 3.7 reshape.101.lower_ref
  20.7 10.2 %shard_map.130 = (f32[8,1088,128]{2,1,0:T(8,128)S(1)}, f32[1088,128]{1,0:T(8,128)S(1)}, f32[1,128]{1,0:T(1,128)S(1)}) custom-call(f32[2,1080,135]{2,1,0:T(8,128)S(1)} %bitcast.54, f32[7,270,135]{2,1,0:T(8,128)S(1)} %copy-done.16, f32[7,270,135]{2,1,0:T(8,128)S(1)} %copy-done.15), custom_call_target="tpu_custom_call" | custom-call | tf_op jit(solution)/shard_map/pallas_call | solution.py:39
  30.9 2.1 copy-done.2
  35.3 10.2 %shard_map.131 = (f32[8,1088,128]{2,1,0:T(8,128)S(1)}, f32[1088,128]{1,0:T(8,128)S(1)}, f32[1,128]{1,0:T(1,128)S(1)}) custom-call(f32[2,1080,135]{2,1,0:T(8,128)S(1)} %bitcast.55, f32[7,270,135]{2,1,0:T(8,128)S(1)} %copy-done.16, f32[7,270,135]{2,1,0:T(8,128)S(1)} %copy-done.15), custom_call_target="tpu_custom_call" | custom-call | tf_op jit(solution)/shard_map/pallas_call | solution.py:39
  45.6 1.9 collective-permute-start.68
  47.7 3.0 collective-permute-start.66
  50.8 7.6 %shard_map.132 = (f32[7,135,16,128]{3,2,1,0:T(8,128)S(1)}, f32[135,16,128]{2,1,0:T(8,128)S(1)}, f32[1,128]{1,0:T(1,128)S(1)}) custom-call(f32[7,135,16,135]{3,2,1,0:T(8,128)} %bitcast.52), custom_call_target="tpu_custom_call" | custom-call | tf_op jit(solution)/shard_map/pallas_call | solution.py:39
  58.3 3.1 copy-done
  61.5 4.6 %collective-permute-start.71 = (f32[1,128]{1,0:T(1,128)S(1)}, f32[1,128]{1,0:T(1,128)S(1)}, u32[]{:S(2)}, u32[]{:S(2)}) collective-permute-start(f32[1,128]{1,0:T(1,128)S(1)} %add_add_fusion.18), channel_id=1, source_target_pairs={{192,0},{193,1},{194,2},{195,3},{196,4},{197,5},{198,6},{199,7},{2... | collective-permute-start | bytes 1544 | tf_op jit(solution)/shard_map/ppermute | solution.py:495
  68.6 5.0 %collective-permute-done.70 = f32[1,128]{1,0:T(1,128)S(1)} collective-permute-done((f32[1,128]{1,0:T(1,128)S(1)}, f32[1,128]{1,0:T(1,128)S(1)}, u32[]{:S(2)}, u32[]{:S(2)}) %collective-permute-start.70) | collective-permute-done | bytes 544 | tf_op jit(solution)/shard_map/ppermute | solution.py:495
  75.8 2.9 collective-permute-start.73
  80.1 2.4 collective-permute-done.72
  84.5 1.9 collective-permute-done.75.refs_0_
  86.4 2.3 copy-done.3
  88.6 2.3 copy-done.6
  93.3 3.9 collective-permute-start.78
  107.6 3.2 copy-done.1
  112.6 2.7 collective-permute-start.85
  121.0 1.9 collective-permute-done.87.refs_0_
  122.9 2.3 copy-done.4
  128.2 2.7 collective-permute-start.90
  134.7 3.3 collective-permute-start.95
  140.5 3.6 collective-permute-done.93.refs_1_
  147.1 2.7 collective-permute-start.97
  155.6 1.9 collective-permute-done.99.refs_0_
  160.5 2.7 collective-permute-start.102
  167.0 2.0 collective-permute-start.107
  171.5 3.4 collective-permute-done.105.refs_1_
  178.4 2.7 collective-permute-start.109
  186.9 1.9 collective-permute-done.111.refs_0_
  191.7 2.7 collective-permute-start.114
  198.2 2.1 collective-permute-start.119
  202.8 3.4 collective-permute-done.117.refs_1_
  209.3 2.7 collective-permute-start.121
  217.8 2.0 collective-permute-done.123.refs_0_
  222.8 2.7 collective-permute-start.126
  229.3 2.1 collective-permute-start.131
  233.9 3.4 collective-permute-done.129.refs_1_
  240.4 2.7 collective-permute-start.133
  248.9 1.9 collective-permute-done.135.refs_0_
  253.8 2.7 collective-permute-start.138
  260.4 2.1 collective-permute-start.143
  265.1 3.4 collective-permute-done.141.refs_1_
  271.6 2.7 collective-permute-start.145
  280.0 1.9 collective-permute-done.147.refs_0_
  284.9 2.5 collective-permute-start.150
  291.2 3.1 collective-permute-start.155
  296.8 3.4 collective-permute-done.153.refs_1_
  303.8 2.7 collective-permute-start.157
  312.2 2.0 collective-permute-done.159.refs_0_
  317.0 2.7 collective-permute-start.162
  323.4 3.9 collective-permute-start.167
  329.9 3.4 collective-permute-done.165.refs_1_
  341.3 2.0 collective-permute-done.169
  347.2 7.5 %collective-permute-start.176 = (f32[16,128]{1,0:T(8,128)S(1)}, f32[16,128]{1,0:T(8,128)S(1)}, u32[]{:S(2)}, u32[]{:S(2)}) collective-permute-start(f32[16,128]{1,0:T(8,128)S(1)} %add_add_fusion.14), channel_id=1, source_target_pairs={{48,0},{49,1},{50,2},{51,3},{52,4},{53,5},{54,6},{55,7},{56,8},{57... | collective-permute-start | bytes 24584 | tf_op jit(solution)/shard_map/ppermute | solution.py:495
  354.7 8.4 %collective-permute-start.175 = (f32[16,128]{1,0:T(8,128)S(1)}, f32[16,128]{1,0:T(8,128)S(1)}, u32[]{:S(2)}, u32[]{:S(2)}) collective-permute-start(f32[16,128]{1,0:T(8,128)S(1)} %add_add_fusion.14), channel_id=1, source_target_pairs={{32,0},{33,1},{34,2},{35,3},{36,4},{37,5},{38,6},{39,7},{40,8},{41... | collective-permute-start | bytes 24584 | tf_op jit(solution)/shard_map/ppermute | solution.py:495
  363.1 2.9 collective-permute-start.174
  366.0 2.3 collective-permute-done.174
  368.2 7.1 %collective-permute-start.179 = (f32[16,128]{1,0:T(8,128)S(1)}, f32[16,128]{1,0:T(8,128)S(1)}, u32[]{:S(2)}, u32[]{:S(2)}) collective-permute-start(f32[16,128]{1,0:T(8,128)S(1)} %add_add_fusion.13), channel_id=1, source_target_pairs={{192,0},{193,1},{194,2},{195,3},{196,4},{197,5},{198,6},{199,7},{2... | collective-permute-start | bytes 24584 | tf_op jit(solution)/shard_map/ppermute | solution.py:495
  375.3 2.7 collective-permute-start.178
  378.1 4.8 %collective-permute-done.178 = f32[16,128]{1,0:T(8,128)S(1)} collective-permute-done((f32[16,128]{1,0:T(8,128)S(1)}, f32[16,128]{1,0:T(8,128)S(1)}, u32[]{:S(2)}, u32[]{:S(2)}) %collective-permute-start.178) | collective-permute-done | bytes 8224 | tf_op jit(solution)/shard_map/ppermute | solution.py:495
  382.9 4.3 %shard_map.150 = (f32[9,16,135]{2,1,0:T(8,128)}, f32[8,128]{1,0:T(8,128)S(1)}, f32[1,128]{1,0:T(1,128)S(1)}, f32[1,128]{1,0:T(1,128)S(1)}) custom-call(f32[16,128]{1,0:T(8,128)S(1)} %add_add_fusion.12.refs_0_, f32[1,128]{1,0:T(1,128)S(1)} %add_add_fusion.17.parts_ref.refs_6_.refs_14_.refs_1_, f32[16,135]{1,0:T(8,128)S(1)} %get-tuple-element.193.refs_5_.refs_2_, ...), custom_call_target="tpu_custom_call" | custom-call | tf_op jit(solution)/shard_map/pallas_call | solution.py:39
  (298 shorter events, 173.5 us)
Async XLA Ops:
  4.4 28.7 %collective-permute-start.62 = (f32[1,128]{1,0:T(1,128)S(1)}, f32[1,128]{1,0:T(1,128)S(1)}, u32[]{:S(2)}, u32[]{:S(2)}) collective-permute-start(f32[1,128]{1,0:T(1,128)S(1)} %shard_map.129), channel_id=1, source_target_pairs={{3,0},{2,1},{1,2},{0,3},{7,4},{6,5},{5,6},{4,7},{11,8},{10,9},{9,1... | collective-permute-start | bytes 1544 | tf_op jit(solution)/shard_map/ppermute | solution.py:495
  7.4 25.6 %collective-permute-start.61 = (f32[1,128]{1,0:T(1,128)S(1)}, f32[1,128]{1,0:T(1,128)S(1)}, u32[]{:S(2)}, u32[]{:S(2)}) collective-permute-start(f32[1,128]{1,0:T(1,128)S(1)} %shard_map.129), channel_id=1, source_target_pairs={{2,0},{3,1},{0,2},{1,3},{6,4},{7,5},{4,6},{5,7},{10,8},{11,9},{8,1... | collective-permute-start | bytes 1544 | tf_op jit(solution)/shard_map/ppermute | solution.py:495
  8.0 25.0 %collective-permute-start.60 = (f32[1,128]{1,0:T(1,128)S(1)}, f32[1,128]{1,0:T(1,128)S(1)}, u32[]{:S(2)}, u32[]{:S(2)}) collective-permute-start(f32[1,128]{1,0:T(1,128)S(1)} %shard_map.129), channel_id=1, source_target_pairs={{1,0},{0,1},{3,2},{2,3},{5,4},{4,5},{7,6},{6,7},{9,8},{8,9},{11,10... | collective-permute-start | bytes 1544 | tf_op jit(solution)/shard_map/ppermute | solution.py:495
  33.0 12.5 %collective-permute-start.65 = (f32[1,128]{1,0:T(1,128)S(1)}, f32[1,128]{1,0:T(1,128)S(1)}, u32[]{:S(2)}, u32[]{:S(2)}) collective-permute-start(f32[1,128]{1,0:T(1,128)S(1)} %add_add_fusion.20), channel_id=1, source_target_pairs={{12,0},{13,1},{14,2},{15,3},{8,4},{9,5},{10,6},{11,7},{4,8},{5,9},... | collective-permute-start | bytes 1544 | tf_op jit(solution)/shard_map/ppermute | solution.py:495
  33.1 12.4 %collective-permute-start.64 = (f32[1,128]{1,0:T(1,128)S(1)}, f32[1,128]{1,0:T(1,128)S(1)}, u32[]{:S(2)}, u32[]{:S(2)}) collective-permute-start(f32[1,128]{1,0:T(1,128)S(1)} %add_add_fusion.20), channel_id=1, source_target_pairs={{8,0},{9,1},{10,2},{11,3},{12,4},{13,5},{14,6},{15,7},{0,8},{1,9},... | collective-permute-start | bytes 1544 | tf_op jit(solution)/shard_map/ppermute | solution.py:495
  34.4 11.2 %collective-permute-start.63 = (f32[1,128]{1,0:T(1,128)S(1)}, f32[1,128]{1,0:T(1,128)S(1)}, u32[]{:S(2)}, u32[]{:S(2)}) collective-permute-start(f32[1,128]{1,0:T(1,128)S(1)} %add_add_fusion.20), channel_id=1, source_target_pairs={{4,0},{5,1},{6,2},{7,3},{0,4},{1,5},{2,6},{3,7},{12,8},{13,9},{14,... | collective-permute-start | bytes 1544 | tf_op jit(solution)/shard_map/ppermute | solution.py:495
  45.6 15.9 %collective-permute-start.68 = (f32[1,128]{1,0:T(1,128)S(1)}, f32[1,128]{1,0:T(1,128)S(1)}, u32[]{:S(2)}, u32[]{:S(2)}) collective-permute-start(f32[1,128]{1,0:T(1,128)S(1)} %add_add_fusion.19), channel_id=1, source_target_pairs={{48,0},{49,1},{50,2},{51,3},{52,4},{53,5},{54,6},{55,7},{56,8},{57... | collective-permute-start | bytes 1544 | tf_op jit(solution)/shard_map/ppermute | solution.py:495
  47.6 13.9 %collective-permute-start.67 = (f32[1,128]{1,0:T(1,128)S(1)}, f32[1,128]{1,0:T(1,128)S(1)}, u32[]{:S(2)}, u32[]{:S(2)}) collective-permute-start(f32[1,128]{1,0:T(1,128)S(1)} %add_add_fusion.19), channel_id=1, source_target_pairs={{32,0},{33,1},{34,2},{35,3},{36,4},{37,5},{38,6},{39,7},{40,8},{41... | collective-permute-start | bytes 1544 | tf_op jit(solution)/shard_map/ppermute | solution.py:495
  47.7 13.8 %collective-permute-start.66 = (f32[1,128]{1,0:T(1,128)S(1)}, f32[1,128]{1,0:T(1,128)S(1)}, u32[]{:S(2)}, u32[]{:S(2)}) collective-permute-start(f32[1,128]{1,0:T(1,128)S(1)} %add_add_fusion.19), channel_id=1, source_target_pairs={{16,0},{17,1},{18,2},{19,3},{20,4},{21,5},{22,6},{23,7},{24,8},{25... | collective-permute-start | bytes 1544 | tf_op jit(solution)/shard_map/ppermute | solution.py:495
  61.5 7.0 %collective-permute-start.71 = (f32[1,128]{1,0:T(1,128)S(1)}, f32[1,128]{1,0:T(1,128)S(1)}, u32[]{:S(2)}, u32[]{:S(2)}) collective-permute-start(f32[1,128]{1,0:T(1,128)S(1)} %add_add_fusion.18), channel_id=1, source_target_pairs={{192,0},{193,1},{194,2},{195,3},{196,4},{197,5},{198,6},{199,7},{2... | collective-permute-start | bytes 1544 | tf_op jit(solution)/shard_map/ppermute | solution.py:495
  66.1 7.4 %collective-permute-start.70 = (f32[1,128]{1,0:T(1,128)S(1)}, f32[1,128]{1,0:T(1,128)S(1)}, u32[]{:S(2)}, u32[]{:S(2)}) collective-permute-start(f32[1,128]{1,0:T(1,128)S(1)} %add_add_fusion.18), channel_id=1, source_target_pairs={{128,0},{129,1},{130,2},{131,3},{132,4},{133,5},{134,6},{135,7},{1... | collective-permute-start | bytes 1544 | tf_op jit(solution)/shard_map/ppermute | solution.py:495
  67.1 6.4 %collective-permute-start.69 = (f32[1,128]{1,0:T(1,128)S(1)}, f32[1,128]{1,0:T(1,128)S(1)}, u32[]{:S(2)}, u32[]{:S(2)}) collective-permute-start(f32[1,128]{1,0:T(1,128)S(1)} %add_add_fusion.18), channel_id=1, source_target_pairs={{64,0},{65,1},{66,2},{67,3},{68,4},{69,5},{70,6},{71,7},{72,8},{73... | collective-permute-start | bytes 1544 | tf_op jit(solution)/shard_map/ppermute | solution.py:495
  74.3 8.2 %collective-permute-start.74 = (f32[16,135]{1,0:T(8,128)S(1)}, f32[16,135]{1,0:T(8,128)S(1)}, u32[]{:S(2)}, u32[]{:S(2)}) collective-permute-start(f32[16,135]{1,0:T(8,128)S(1)} %get-tuple-element.193.refs_5_.refs_2_), channel_id=1, source_target_pairs={{3,0},{0,1},{1,2},{2,3},{7,4},{4,5},{5,6},{6,7},{11,8},{8,9},{9,10... | collective-permute-start | bytes 25928 | tf_op jit(solution)/shard_map/ppermute | solution.py:478
  75.8 6.6 %collective-permute-start.73 = (f32[16,135]{1,0:T(8,128)S(1)}, f32[16,135]{1,0:T(8,128)S(1)}, u32[]{:S(2)}, u32[]{:S(2)}) collective-permute-start(f32[16,135]{1,0:T(8,128)S(1)} %get-tuple-element.193.refs_5_.refs_2_), channel_id=1, source_target_pairs={{2,0},{3,1},{0,2},{1,3},{6,4},{7,5},{4,6},{5,7},{10,8},{11,9},{8,1... | collective-permute-start | bytes 25928 | tf_op jit(solution)/shard_map/ppermute | solution.py:478
  92.5 5.6 %collective-permute-start.79 = (f32[16,135]{1,0:T(8,128)S(1)}, f32[16,135]{1,0:T(8,128)S(1)}, u32[]{:S(2)}, u32[]{:S(2)}) collective-permute-start(f32[16,135]{1,0:T(8,128)S(1)} %shard_map.134), channel_id=1, source_target_pairs={{3,0},{0,1},{1,2},{2,3},{7,4},{4,5},{5,6},{6,7},{11,8},{8,9},{9,10... | collective-permute-start | bytes 25928 | tf_op jit(solution)/shard_map/ppermute | solution.py:478
  93.3 5.8 %collective-permute-start.78 = (f32[16,135]{1,0:T(8,128)S(1)}, f32[16,135]{1,0:T(8,128)S(1)}, u32[]{:S(2)}, u32[]{:S(2)}) collective-permute-start(f32[16,135]{1,0:T(8,128)S(1)} %shard_map.134), channel_id=1, source_target_pairs={{2,0},{3,1},{0,2},{1,3},{6,4},{7,5},{4,6},{5,7},{10,8},{11,9},{8,1... | collective-permute-start | bytes 25928 | tf_op jit(solution)/shard_map/ppermute | solution.py:478
  102.0 5.5 %collective-permute-start.80 = (f32[64,135]{1,0:T(8,128)S(1)}, f32[64,135]{1,0:T(8,128)S(1)}, u32[]{:S(2)}, u32[]{:S(2)}) collective-permute-start(f32[64,135]{1,0:T(8,128)S(1)} %pad_maximum_fusion.2.refs_2_), channel_id=1, source_target_pairs={{248,0},{249,1},{250,2},{251,3},{252,4},{253,5},{254,6},{255,7},{0... | collective-permute-start | bytes 103688 | tf_op jit(solution)/shard_map/ppermute | solution.py:478
  112.5 5.0 %collective-permute-start.86 = (f32[16,135]{1,0:T(8,128)S(1)}, f32[16,135]{1,0:T(8,128)S(1)}, u32[]{:S(2)}, u32[]{:S(2)}) collective-permute-start(f32[16,135]{1,0:T(8,128)S(1)} %shard_map.135.refs_5_.refs_6_.refs_3_), channel_id=1, source_target_pairs={{3,0},{0,1},{1,2},{2,3},{7,4},{4,5},{5,6},{6,7},{11,8},{8,9},{9,10... | collective-permute-start | bytes 25928 | tf_op jit(solution)/shard_map/ppermute | solution.py:478
  112.6 5.3 %collective-permute-start.85 = (f32[16,135]{1,0:T(8,128)S(1)}, f32[16,135]{1,0:T(8,128)S(1)}, u32[]{:S(2)}, u32[]{:S(2)}) collective-permute-start(f32[16,135]{1,0:T(8,128)S(1)} %shard_map.135.refs_5_.refs_6_.refs_3_), channel_id=1, source_target_pairs={{2,0},{3,1},{0,2},{1,3},{6,4},{7,5},{4,6},{5,7},{10,8},{11,9},{8,1... | collective-permute-start | bytes 25928 | tf_op jit(solution)/shard_map/ppermute | solution.py:478
  126.8 5.0 %collective-permute-start.91 = (f32[16,135]{1,0:T(8,128)S(1)}, f32[16,135]{1,0:T(8,128)S(1)}, u32[]{:S(2)}, u32[]{:S(2)}) collective-permute-start(f32[16,135]{1,0:T(8,128)S(1)} %shard_map.136), channel_id=1, source_target_pairs={{3,0},{0,1},{1,2},{2,3},{7,4},{4,5},{5,6},{6,7},{11,8},{8,9},{9,10... | collective-permute-start | bytes 25928 | tf_op jit(solution)/shard_map/ppermute | solution.py:478
  128.2 5.2 %collective-permute-start.90 = (f32[16,135]{1,0:T(8,128)S(1)}, f32[16,135]{1,0:T(8,128)S(1)}, u32[]{:S(2)}, u32[]{:S(2)}) collective-permute-start(f32[16,135]{1,0:T(8,128)S(1)} %shard_map.136), channel_id=1, source_target_pairs={{2,0},{3,1},{0,2},{1,3},{6,4},{7,5},{4,6},{5,7},{10,8},{11,9},{8,1... | collective-permute-start | bytes 25928 | tf_op jit(solution)/shard_map/ppermute | solution.py:478
  134.7 5.2 %collective-permute-start.95 = (f32[64,135]{1,0:T(8,128)S(1)}, f32[64,135]{1,0:T(8,128)S(1)}, u32[]{:S(2)}, u32[]{:S(2)}) collective-permute-start(f32[64,135]{1,0:T(8,128)S(1)} %pad_maximum_fusion.4.refs_2_), channel_id=1, source_target_pairs={{8,0},{9,1},{10,2},{11,3},{12,4},{13,5},{14,6},{15,7},{16,8},{17,9... | collective-permute-start | bytes 103688 | tf_op jit(solution)/shard_map/ppermute | solution.py:478
  138.1 5.9 %collective-permute-start.93 = (f32[64,135]{1,0:T(8,128)S(1)}, f32[64,135]{1,0:T(8,128)S(1)}, u32[]{:S(2)}, u32[]{:S(2)}) collective-permute-start(f32[64,135]{1,0:T(8,128)S(1)} %pad_maximum_fusion.4.refs_2_), channel_id=1, source_target_pairs={{252,0},{253,1},{254,2},{255,3},{0,4},{1,5},{2,6},{3,7},{4,8},{5,9... | collective-permute-start | bytes 103688 | tf_op jit(solution)/shard_map/ppermute | solution.py:478
  138.6 6.7 %collective-permute-start.92 = (f32[64,135]{1,0:T(8,128)S(1)}, f32[64,135]{1,0:T(8,128)S(1)}, u32[]{:S(2)}, u32[]{:S(2)}) collective-permute-start(f32[64,135]{1,0:T(8,128)S(1)} %pad_maximum_fusion.4.refs_2_), channel_id=1, source_target_pairs={{248,0},{249,1},{250,2},{251,3},{252,4},{253,5},{254,6},{255,7},{0... | collective-permute-start | bytes 103688 | tf_op jit(solution)/shard_map/ppermute | solution.py:478
  147.0 5.0 %collective-permute-start.98 = (f32[16,135]{1,0:T(8,128)S(1)}, f32[16,135]{1,0:T(8,128)S(1)}, u32[]{:S(2)}, u32[]{:S(2)}) collective-permute-start(f32[16,135]{1,0:T(8,128)S(1)} %shard_map.137.refs_5_.refs_7_.refs_4_), channel_id=1, source_target_pairs={{3,0},{0,1},{1,2},{2,3},{7,4},{4,5},{5,6},{6,7},{11,8},{8,9},{9,10... | collective-permute-start | bytes 25928 | tf_op jit(solution)/shard_map/ppermute | solution.py:478
  147.1 5.3 %collective-permute-start.97 = (f32[16,135]{1,0:T(8,128)S(1)}, f32[16,135]{1,0:T(8,128)S(1)}, u32[]{:S(2)}, u32[]{:S(2)}) collective-permute-start(f32[16,135]{1,0:T(8,128)S(1)} %shard_map.137.refs_5_.refs_7_.refs_4_), channel_id=1, source_target_pairs={{2,0},{3,1},{0,2},{1,3},{6,4},{7,5},{4,6},{5,7},{10,8},{11,9},{8,1... | collective-permute-start | bytes 25928 | tf_op jit(solution)/shard_map/ppermute | solution.py:478
  159.2 5.0 %collective-permute-start.103 = (f32[16,135]{1,0:T(8,128)S(1)}, f32[16,135]{1,0:T(8,128)S(1)}, u32[]{:S(2)}, u32[]{:S(2)}) collective-permute-start(f32[16,135]{1,0:T(8,128)S(1)} %shard_map.138), channel_id=1, source_target_pairs={{3,0},{0,1},{1,2},{2,3},{7,4},{4,5},{5,6},{6,7},{11,8},{8,9},{9,10... | collective-permute-start | bytes 25928 | tf_op jit(solution)/shard_map/ppermute | solution.py:478
  160.5 5.2 %collective-permute-start.102 = (f32[16,135]{1,0:T(8,128)S(1)}, f32[16,135]{1,0:T(8,128)S(1)}, u32[]{:S(2)}, u32[]{:S(2)}) collective-permute-start(f32[16,135]{1,0:T(8,128)S(1)} %shard_map.138), channel_id=1, source_target_pairs={{2,0},{3,1},{0,2},{1,3},{6,4},{7,5},{4,6},{5,7},{10,8},{11,9},{8,1... | collective-permute-start | bytes 25928 | tf_op jit(solution)/shard_map/ppermute | solution.py:478
  169.0 5.9 %collective-permute-start.105 = (f32[64,135]{1,0:T(8,128)S(1)}, f32[64,135]{1,0:T(8,128)S(1)}, u32[]{:S(2)}, u32[]{:S(2)}) collective-permute-start(f32[64,135]{1,0:T(8,128)S(1)} %pad_maximum_fusion.6.refs_2_), channel_id=1, source_target_pairs={{252,0},{253,1},{254,2},{255,3},{0,4},{1,5},{2,6},{3,7},{4,8},{5,9... | collective-permute-start | bytes 103688 | tf_op jit(solution)/shard_map/ppermute | solution.py:478
  169.5 6.7 %collective-permute-start.104 = (f32[64,135]{1,0:T(8,128)S(1)}, f32[64,135]{1,0:T(8,128)S(1)}, u32[]{:S(2)}, u32[]{:S(2)}) collective-permute-start(f32[64,135]{1,0:T(8,128)S(1)} %pad_maximum_fusion.6.refs_2_), channel_id=1, source_target_pairs={{248,0},{249,1},{250,2},{251,3},{252,4},{253,5},{254,6},{255,7},{0... | collective-permute-start | bytes 103688 | tf_op jit(solution)/shard_map/ppermute | solution.py:478
  177.9 5.4 %collective-permute-start.110 = (f32[16,135]{1,0:T(8,128)S(1)}, f32[16,135]{1,0:T(8,128)S(1)}, u32[]{:S(2)}, u32[]{:S(2)}) collective-permute-start(f32[16,135]{1,0:T(8,128)S(1)} %shard_map.139.refs_5_.refs_8_), channel_id=1, source_target_pairs={{3,0},{0,1},{1,2},{2,3},{7,4},{4,5},{5,6},{6,7},{11,8},{8,9},{9,10... | collective-permute-start | bytes 25928 | tf_op jit(solution)/shard_map/ppermute | solution.py:478
  178.4 5.3 %collective-permute-start.109 = (f32[16,135]{1,0:T(8,128)S(1)}, f32[16,135]{1,0:T(8,128)S(1)}, u32[]{:S(2)}, u32[]{:S(2)}) collective-permute-start(f32[16,135]{1,0:T(8,128)S(1)} %shard_map.139.refs_5_.refs_8_), channel_id=1, source_target_pairs={{2,0},{3,1},{0,2},{1,3},{6,4},{7,5},{4,6},{5,7},{10,8},{11,9},{8,1... | collective-permute-start | bytes 25928 | tf_op jit(solution)/shard_map/ppermute | solution.py:478
  190.4 5.0 %collective-permute-start.115 = (f32[16,135]{1,0:T(8,128)S(1)}, f32[16,135]{1,0:T(8,128)S(1)}, u32[]{:S(2)}, u32[]{:S(2)}) collective-permute-start(f32[16,135]{1,0:T(8,128)S(1)} %shard_map.140), channel_id=1, source_target_pairs={{3,0},{0,1},{1,2},{2,3},{7,4},{4,5},{5,6},{6,7},{11,8},{8,9},{9,10... | collective-permute-start | bytes 25928 | tf_op jit(solution)/shard_map/ppermute | solution.py:478
  191.7 5.2 %collective-permute-start.114 = (f32[16,135]{1,0:T(8,128)S(1)}, f32[16,135]{1,0:T(8,128)S(1)}, u32[]{:S(2)}, u32[]{:S(2)}) collective-permute-start(f32[16,135]{1,0:T(8,128)S(1)} %shard_map.140), channel_id=1, source_target_pairs={{2,0},{3,1},{0,2},{1,3},{6,4},{7,5},{4,6},{5,7},{10,8},{11,9},{8,1... | collective-permute-start | bytes 25928 | tf_op jit(solution)/shard_map/ppermute | solution.py:478
  200.3 5.9 %collective-permute-start.117 = (f32[64,135]{1,0:T(8,128)S(1)}, f32[64,135]{1,0:T(8,128)S(1)}, u32[]{:S(2)}, u32[]{:S(2)}) collective-permute-start(f32[64,135]{1,0:T(8,128)S(1)} %pad_maximum_fusion.8.refs_2_), channel_id=1, source_target_pairs={{252,0},{253,1},{254,2},{255,3},{0,4},{1,5},{2,6},{3,7},{4,8},{5,9... | collective-permute-start | bytes 103688 | tf_op jit(solution)/shard_map/ppermute | solution.py:478
  200.8 6.7 %collective-permute-start.116 = (f32[64,135]{1,0:T(8,128)S(1)}, f32[64,135]{1,0:T(8,128)S(1)}, u32[]{:S(2)}, u32[]{:S(2)}) collective-permute-start(f32[64,135]{1,0:T(8,128)S(1)} %pad_maximum_fusion.8.refs_2_), channel_id=1, source_target_pairs={{248,0},{249,1},{250,2},{251,3},{252,4},{253,5},{254,6},{255,7},{0... | collective-permute-start | bytes 103688 | tf_op jit(solution)/shard_map/ppermute | solution.py:478
  209.2 5.0 %collective-permute-start.122 = (f32[16,135]{1,0:T(8,128)S(1)}, f32[16,135]{1,0:T(8,128)S(1)}, u32[]{:S(2)}, u32[]{:S(2)}) collective-permute-start(f32[16,135]{1,0:T(8,128)S(1)} %shard_map.141.refs_5_.refs_9_.refs_6_), channel_id=1, source_target_pairs={{3,0},{0,1},{1,2},{2,3},{7,4},{4,5},{5,6},{6,7},{11,8},{8,9},{9,10... | collective-permute-start | bytes 25928 | tf_op jit(solution)/shard_map/ppermute | solution.py:478
  209.3 5.3 %collective-permute-start.121 = (f32[16,135]{1,0:T(8,128)S(1)}, f32[16,135]{1,0:T(8,128)S(1)}, u32[]{:S(2)}, u32[]{:S(2)}) collective-permute-start(f32[16,135]{1,0:T(8,128)S(1)} %shard_map.141.refs_5_.refs_9_.refs_6_), channel_id=1, source_target_pairs={{2,0},{3,1},{0,2},{1,3},{6,4},{7,5},{4,6},{5,7},{10,8},{11,9},{8,1... | collective-permute-start | bytes 25928 | tf_op jit(solution)/shard_map/ppermute | solution.py:478
  222.8 5.2 %collective-permute-start.126 = (f32[16,135]{1,0:T(8,128)S(1)}, f32[16,135]{1,0:T(8,128)S(1)}, u32[]{:S(2)}, u32[]{:S(2)}) collective-permute-start(f32[16,135]{1,0:T(8,128)S(1)} %shard_map.142), channel_id=1, source_target_pairs={{2,0},{3,1},{0,2},{1,3},{6,4},{7,5},{4,6},{5,7},{10,8},{11,9},{8,1... | collective-permute-start | bytes 25928 | tf_op jit(solution)/shard_map/ppermute | solution.py:478
  231.4 6.0 %collective-permute-start.129 = (f32[64,135]{1,0:T(8,128)S(1)}, f32[64,135]{1,0:T(8,128)S(1)}, u32[]{:S(2)}, u32[]{:S(2)}) collective-permute-start(f32[64,135]{1,0:T(8,128)S(1)} %pad_maximum_fusion.10.refs_2_), channel_id=1, source_target_pairs={{252,0},{253,1},{254,2},{255,3},{0,4},{1,5},{2,6},{3,7},{4,8},{5,9... | collective-permute-start | bytes 103688 | tf_op jit(solution)/shard_map/ppermute | solution.py:478
  231.9 6.7 %collective-permute-start.128 = (f32[64,135]{1,0:T(8,128)S(1)}, f32[64,135]{1,0:T(8,128)S(1)}, u32[]{:S(2)}, u32[]{:S(2)}) collective-permute-start(f32[64,135]{1,0:T(8,128)S(1)} %pad_maximum_fusion.10.refs_2_), channel_id=1, source_target_pairs={{248,0},{249,1},{250,2},{251,3},{252,4},{253,5},{254,6},{255,7},{0... | collective-permute-start | bytes 103688 | tf_op jit(solution)/shard_map/ppermute | solution.py:478
  240.3 5.0 %collective-permute-start.134 = (f32[16,135]{1,0:T(8,128)S(1)}, f32[16,135]{1,0:T(8,128)S(1)}, u32[]{:S(2)}, u32[]{:S(2)}) collective-permute-start(f32[16,135]{1,0:T(8,128)S(1)} %shard_map.143.refs_5_.refs_10_.refs_7_), channel_id=1, source_target_pairs={{3,0},{0,1},{1,2},{2,3},{7,4},{4,5},{5,6},{6,7},{11,8},{8,9},{9,10... | collective-permute-start | bytes 25928 | tf_op jit(solution)/shard_map/ppermute | solution.py:478
  240.4 5.3 %collective-permute-start.133 = (f32[16,135]{1,0:T(8,128)S(1)}, f32[16,135]{1,0:T(8,128)S(1)}, u32[]{:S(2)}, u32[]{:S(2)}) collective-permute-start(f32[16,135]{1,0:T(8,128)S(1)} %shard_map.143.refs_5_.refs_10_.refs_7_), channel_id=1, source_target_pairs={{2,0},{3,1},{0,2},{1,3},{6,4},{7,5},{4,6},{5,7},{10,8},{11,9},{8,1... | collective-permute-start | bytes 25928 | tf_op jit(solution)/shard_map/ppermute | solution.py:478
  253.8 5.2 %collective-permute-start.138 = (f32[16,135]{1,0:T(8,128)S(1)}, f32[16,135]{1,0:T(8,128)S(1)}, u32[]{:S(2)}, u32[]{:S(2)}) collective-permute-start(f32[16,135]{1,0:T(8,128)S(1)} %shard_map.144), channel_id=1, source_target_pairs={{2,0},{3,1},{0,2},{1,3},{6,4},{7,5},{4,6},{5,7},{10,8},{11,9},{8,1... | collective-permute-start | bytes 25928 | tf_op jit(solution)/shard_map/ppermute | solution.py:478
  262.5 5.9 %collective-permute-start.141 = (f32[64,135]{1,0:T(8,128)S(1)}, f32[64,135]{1,0:T(8,128)S(1)}, u32[]{:S(2)}, u32[]{:S(2)}) collective-permute-start(f32[64,135]{1,0:T(8,128)S(1)} %pad_maximum_fusion.12.refs_2_), channel_id=1, source_target_pairs={{252,0},{253,1},{254,2},{255,3},{0,4},{1,5},{2,6},{3,7},{4,8},{5,9... | collective-permute-start | bytes 103688 | tf_op jit(solution)/shard_map/ppermute | solution.py:478
  263.0 6.7 %collective-permute-start.140 = (f32[64,135]{1,0:T(8,128)S(1)}, f32[64,135]{1,0:T(8,128)S(1)}, u32[]{:S(2)}, u32[]{:S(2)}) collective-permute-start(f32[64,135]{1,0:T(8,128)S(1)} %pad_maximum_fusion.12.refs_2_), channel_id=1, source_target_pairs={{248,0},{249,1},{250,2},{251,3},{252,4},{253,5},{254,6},{255,7},{0... | collective-permute-start | bytes 103688 | tf_op jit(solution)/shard_map/ppermute | solution.py:478
  271.4 5.0 %collective-permute-start.146 = (f32[16,135]{1,0:T(8,128)S(1)}, f32[16,135]{1,0:T(8,128)S(1)}, u32[]{:S(2)}, u32[]{:S(2)}) collective-permute-start(f32[16,135]{1,0:T(8,128)S(1)} %shard_map.145.refs_5_.refs_11_.refs_8_), channel_id=1, source_target_pairs={{3,0},{0,1},{1,2},{2,3},{7,4},{4,5},{5,6},{6,7},{11,8},{8,9},{9,10... | collective-permute-start | bytes 25928 | tf_op jit(solution)/shard_map/ppermute | solution.py:478
  271.6 5.3 %collective-permute-start.145 = (f32[16,135]{1,0:T(8,128)S(1)}, f32[16,135]{1,0:T(8,128)S(1)}, u32[]{:S(2)}, u32[]{:S(2)}) collective-permute-start(f32[16,135]{1,0:T(8,128)S(1)} %shard_map.145.refs_5_.refs_11_.refs_8_), channel_id=1, source_target_pairs={{2,0},{3,1},{0,2},{1,3},{6,4},{7,5},{4,6},{5,7},{10,8},{11,9},{8,1... | collective-permute-start | bytes 25928 | tf_op jit(solution)/shard_map/ppermute | solution.py:478
  284.9 5.2 %collective-permute-start.150 = (f32[16,135]{1,0:T(8,128)S(1)}, f32[16,135]{1,0:T(8,128)S(1)}, u32[]{:S(2)}, u32[]{:S(2)}) collective-permute-start(f32[16,135]{1,0:T(8,128)S(1)} %shard_map.146), channel_id=1, source_target_pairs={{2,0},{3,1},{0,2},{1,3},{6,4},{7,5},{4,6},{5,7},{10,8},{11,9},{8,1... | collective-permute-start | bytes 25928 | tf_op jit(solution)/shard_map/ppermute | solution.py:478
  291.2 5.0 %collective-permute-start.155 = (f32[64,135]{1,0:T(8,128)S(1)}, f32[64,135]{1,0:T(8,128)S(1)}, u32[]{:S(2)}, u32[]{:S(2)}) collective-permute-start(f32[64,135]{1,0:T(8,128)S(1)} %pad_maximum_fusion.14.refs_2_), channel_id=1, source_target_pairs={{8,0},{9,1},{10,2},{11,3},{12,4},{13,5},{14,6},{15,7},{16,8},{17,9... | collective-permute-start | bytes 103688 | tf_op jit(solution)/shard_map/ppermute | solution.py:478
  294.3 5.9 %collective-permute-start.153 = (f32[64,135]{1,0:T(8,128)S(1)}, f32[64,135]{1,0:T(8,128)S(1)}, u32[]{:S(2)}, u32[]{:S(2)}) collective-permute-start(f32[64,135]{1,0:T(8,128)S(1)} %pad_maximum_fusion.14.refs_2_), channel_id=1, source_target_pairs={{252,0},{253,1},{254,2},{255,3},{0,4},{1,5},{2,6},{3,7},{4,8},{5,9... | collective-permute-start | bytes 103688 | tf_op jit(solution)/shard_map/ppermute | solution.py:478
  294.8 6.8 %collective-permute-start.152 = (f32[64,135]{1,0:T(8,128)S(1)}, f32[64,135]{1,0:T(8,128)S(1)}, u32[]{:S(2)}, u32[]{:S(2)}) collective-permute-start(f32[64,135]{1,0:T(8,128)S(1)} %pad_maximum_fusion.14.refs_2_), channel_id=1, source_target_pairs={{248,0},{249,1},{250,2},{251,3},{252,4},{253,5},{254,6},{255,7},{0... | collective-permute-start | bytes 103688 | tf_op jit(solution)/shard_map/ppermute | solution.py:478
  303.2 5.0 %collective-permute-start.158 = (f32[16,135]{1,0:T(8,128)S(1)}, f32[16,135]{1,0:T(8,128)S(1)}, u32[]{:S(2)}, u32[]{:S(2)}) collective-permute-start(f32[16,135]{1,0:T(8,128)S(1)} %shard_map.147.refs_12_.refs_13_.refs_9_), channel_id=1, source_target_pairs={{3,0},{0,1},{1,2},{2,3},{7,4},{4,5},{5,6},{6,7},{11,8},{8,9},{9,10... | collective-permute-start | bytes 25928 | tf_op jit(solution)/shard_map/ppermute | solution.py:478
  303.8 5.2 %collective-permute-start.157 = (f32[16,135]{1,0:T(8,128)S(1)}, f32[16,135]{1,0:T(8,128)S(1)}, u32[]{:S(2)}, u32[]{:S(2)}) collective-permute-start(f32[16,135]{1,0:T(8,128)S(1)} %shard_map.147.refs_12_.refs_13_.refs_9_), channel_id=1, source_target_pairs={{2,0},{3,1},{0,2},{1,3},{6,4},{7,5},{4,6},{5,7},{10,8},{11,9},{8,1... | collective-permute-start | bytes 25928 | tf_op jit(solution)/shard_map/ppermute | solution.py:478
  317.0 5.2 %collective-permute-start.162 = (f32[16,135]{1,0:T(8,128)S(1)}, f32[16,135]{1,0:T(8,128)S(1)}, u32[]{:S(2)}, u32[]{:S(2)}) collective-permute-start(f32[16,135]{1,0:T(8,128)S(1)} %shard_map.148), channel_id=1, source_target_pairs={{2,0},{3,1},{0,2},{1,3},{6,4},{7,5},{4,6},{5,7},{10,8},{11,9},{8,1... | collective-permute-start | bytes 25928 | tf_op jit(solution)/shard_map/ppermute | solution.py:478
  323.4 5.8 %collective-permute-start.167 = (f32[64,135]{1,0:T(8,128)S(1)}, f32[64,135]{1,0:T(8,128)S(1)}, u32[]{:S(2)}, u32[]{:S(2)}) collective-permute-start(f32[64,135]{1,0:T(8,128)S(1)} %pad_maximum_fusion.16.refs_2_), channel_id=1, source_target_pairs={{8,0},{9,1},{10,2},{11,3},{12,4},{13,5},{14,6},{15,7},{16,8},{17,9... | collective-permute-start | bytes 103688 | tf_op jit(solution)/shard_map/ppermute | solution.py:478
  327.3 5.9 %collective-permute-start.165 = (f32[64,135]{1,0:T(8,128)S(1)}, f32[64,135]{1,0:T(8,128)S(1)}, u32[]{:S(2)}, u32[]{:S(2)}) collective-permute-start(f32[64,135]{1,0:T(8,128)S(1)} %pad_maximum_fusion.16.refs_2_), channel_id=1, source_target_pairs={{252,0},{253,1},{254,2},{255,3},{0,4},{1,5},{2,6},{3,7},{4,8},{5,9... | collective-permute-start | bytes 103688 | tf_op jit(solution)/shard_map/ppermute | solution.py:478
  327.8 6.7 %collective-permute-start.164 = (f32[64,135]{1,0:T(8,128)S(1)}, f32[64,135]{1,0:T(8,128)S(1)}, u32[]{:S(2)}, u32[]{:S(2)}) collective-permute-start(f32[64,135]{1,0:T(8,128)S(1)} %pad_maximum_fusion.16.refs_2_), channel_id=1, source_target_pairs={{248,0},{249,1},{250,2},{251,3},{252,4},{253,5},{254,6},{255,7},{0... | collective-permute-start | bytes 103688 | tf_op jit(solution)/shard_map/ppermute | solution.py:478
  338.2 5.2 %collective-permute-start.169 = (f32[16,128]{1,0:T(8,128)S(1)}, f32[16,128]{1,0:T(8,128)S(1)}, u32[]{:S(2)}, u32[]{:S(2)}) collective-permute-start(f32[16,128]{1,0:T(8,128)S(1)} %get-tuple-element.200), channel_id=1, source_target_pairs={{2,0},{3,1},{0,2},{1,3},{6,4},{7,5},{4,6},{5,7},{10,8},{11,9},{8,1... | collective-permute-start | bytes 24584 | tf_op jit(solution)/shard_map/ppermute | solution.py:495
  347.2 18.8 %collective-permute-start.176 = (f32[16,128]{1,0:T(8,128)S(1)}, f32[16,128]{1,0:T(8,128)S(1)}, u32[]{:S(2)}, u32[]{:S(2)}) collective-permute-start(f32[16,128]{1,0:T(8,128)S(1)} %add_add_fusion.14), channel_id=1, source_target_pairs={{48,0},{49,1},{50,2},{51,3},{52,4},{53,5},{54,6},{55,7},{56,8},{57... | collective-permute-start | bytes 24584 | tf_op jit(solution)/shard_map/ppermute | solution.py:495
  354.7 11.2 %collective-permute-start.175 = (f32[16,128]{1,0:T(8,128)S(1)}, f32[16,128]{1,0:T(8,128)S(1)}, u32[]{:S(2)}, u32[]{:S(2)}) collective-permute-start(f32[16,128]{1,0:T(8,128)S(1)} %add_add_fusion.14), channel_id=1, source_target_pairs={{32,0},{33,1},{34,2},{35,3},{36,4},{37,5},{38,6},{39,7},{40,8},{41... | collective-permute-start | bytes 24584 | tf_op jit(solution)/shard_map/ppermute | solution.py:495
  363.1 5.2 %collective-permute-start.174 = (f32[16,128]{1,0:T(8,128)S(1)}, f32[16,128]{1,0:T(8,128)S(1)}, u32[]{:S(2)}, u32[]{:S(2)}) collective-permute-start(f32[16,128]{1,0:T(8,128)S(1)} %add_add_fusion.14), channel_id=1, source_target_pairs={{16,0},{17,1},{18,2},{19,3},{20,4},{21,5},{22,6},{23,7},{24,8},{25... | collective-permute-start | bytes 24584 | tf_op jit(solution)/shard_map/ppermute | solution.py:495
  368.2 9.8 %collective-permute-start.179 = (f32[16,128]{1,0:T(8,128)S(1)}, f32[16,128]{1,0:T(8,128)S(1)}, u32[]{:S(2)}, u32[]{:S(2)}) collective-permute-start(f32[16,128]{1,0:T(8,128)S(1)} %add_add_fusion.13), channel_id=1, source_target_pairs={{192,0},{193,1},{194,2},{195,3},{196,4},{197,5},{198,6},{199,7},{2... | collective-permute-start | bytes 24584 | tf_op jit(solution)/shard_map/ppermute | solution.py:495
  375.3 7.6 %collective-permute-start.178 = (f32[16,128]{1,0:T(8,128)S(1)}, f32[16,128]{1,0:T(8,128)S(1)}, u32[]{:S(2)}, u32[]{:S(2)}) collective-permute-start(f32[16,128]{1,0:T(8,128)S(1)} %add_add_fusion.13), channel_id=1, source_target_pairs={{128,0},{129,1},{130,2},{131,3},{132,4},{133,5},{134,6},{135,7},{1... | collective-permute-start | bytes 24584 | tf_op jit(solution)/shard_map/ppermute | solution.py:495
  (80 other events, 473.9 us)
